TPU v7x, 128 devices: a whole 4x4x4 slice. The times are simulated.
128 devices in a mesh: chan: 8 (over y, core), tm: 16 (over x, z).
Axes of the slice: x: 4, y: 4, z: 4, core: 2. Of those that a mesh axis runs over, the one named last changes fastest.
Arguments:
- readings: float32 [16384, 16384], P('chan', 'tm'), may hold values from -8 to 8
- channel_start: float32 [16384, 64], P(('chan', 'tm')), may hold values from -6 to 6
- time_start: float32 [16384, 64], P(('tm', 'chan')), may hold values from -0.75 to 0.75
Outputs:
- outliers: float32 [16384, 16384], P('chan', 'tm')
- channel_factors: float32 [16384, 64], P(('chan', 'tm'))
- time_factors: float32 [16384, 64], P(('tm', 'chan'))
All inputs are finite; a program needn't handle non-finite values.
Results may differ from a plain program's by a relative error of at most 0.00019.
Values sent between devices are 32-bit elements; how exact they have to be, the bound alone decides.
No kernel may reach another device: no remote copies, remote signals or barrier semaphores. Data moves between devices by JAX's collectives and lax.ppermute only.
A program may use at most 128 MiB of HBM per device.

v0:
```python
import jax
import jax.numpy as jnp
from jax import lax
from jax.sharding import PartitionSpec as P

ITERS = 2


threshold_level = 1.5
ridge_weight = 8.0


def rows_product(first, second):
    return lax.dot_general(
        first,
        second,
        (((1,), (1,)), ((), ())),
        precision=lax.Precision.HIGHEST,
        preferred_element_type=jnp.float32,
    )


def cols_product(first, second):
    return lax.dot_general(
        first,
        second,
        (((0,), (0,)), ((), ())),
        precision=lax.Precision.HIGHEST,
        preferred_element_type=jnp.float32,
    )


def solve_ridge(partial_value, gram):
    factor_chol = jnp.linalg.cholesky(gram)
    middle = lax.linalg.triangular_solve(
        factor_chol, partial_value, left_side=False, lower=True, transpose_a=True
    )
    return lax.linalg.triangular_solve(
        factor_chol, middle, left_side=False, lower=True, transpose_a=False
    )


def gram_sum(piece, identity):
    local_gram = cols_product(piece, piece)
    return lax.psum(local_gram, ("chan", "tm")) + ridge_weight * identity


def gather_left(piece):
    return lax.all_gather(piece, "tm", axis=0, tiled=True)


def gather_right(piece):
    return lax.all_gather(piece, "chan", axis=0, tiled=True)


def shards(readings, channel_start, time_start):
    factor_width = channel_start.shape[1]
    identity = jnp.eye(factor_width, dtype=jnp.float32)
    left_count = channel_start.shape[0]
    right_count = time_start.shape[0]
    left_piece = channel_start
    right_piece = time_start
    left_block = gather_left(left_piece)
    right_block = gather_right(right_piece)
    outliers = readings
    for sweep in range(ITERS):
        residue = readings - rows_product(left_block, right_block)
        outliers = residue - jnp.clip(residue, -threshold_level, threshold_level)
        cleaned = readings - outliers
        gram_right = gram_sum(right_piece, identity)
        left_total = lax.psum(
            jnp.dot(
                cleaned,
                right_block,
                precision=lax.Precision.HIGHEST,
                preferred_element_type=jnp.float32,
            ),
            "tm",
        )
        left_block = solve_ridge(left_total, gram_right)
        left_piece = lax.dynamic_slice_in_dim(
            left_block, lax.axis_index("tm") * left_count, left_count, 0
        )
        gram_left = gram_sum(left_piece, identity)
        right_total = lax.psum(cols_product(cleaned, left_block), "chan")
        right_block = solve_ridge(right_total, gram_left)
        right_piece = lax.dynamic_slice_in_dim(
            right_block, lax.axis_index("chan") * right_count, right_count, 0
        )
    return (outliers, left_piece, right_piece)


def solution(mesh):
    in_specs = (P("chan", "tm"), P(("chan", "tm"), None), P(("tm", "chan"), None))
    out_specs = (P("chan", "tm"), P(("chan", "tm"), None), P(("tm", "chan"), None))
    return jax.shard_map(shards, mesh=mesh, in_specs=in_specs, out_specs=out_specs, check_vma=False)
```

profile of v0, /device:TPU:1, one launch (start us, length us, event | category | flops | bytes accessed | tf_op | source)
XLA Modules:
  0.0 529.7 jit_solution(12258336436494625318)
XLA Ops:
  7.2 14.9 %all_gather.7 = f32[1024,64]{0,1:T(8,128)S(1)} all-gather(f32[128,64]{0,1:T(8,128)} %param.14), channel_id=1, replica_groups=mesh['chan'=8,'tm'=16] {'chan'}, dimensions={0}, use_global_device_ids=true | all-gather | bytes 294912 | tf_op jit(solution)/shard_map/all_gather | solution.py:53
  22.1 21.0 %all_gather.6 = f32[2048,64]{0,1:T(8,128)S(1)} all-gather(f32[128,64]{0,1:T(8,128)} %param.13), channel_id=1, replica_groups=mesh['chan'=8,'tm'=16] {'tm'}, dimensions={0}, use_global_device_ids=true | all-gather | bytes 557056 | tf_op jit(solution)/shard_map/all_gather | solution.py:49
  43.1 9.9 %fusion = f32[2048,1024]{1,0:T(8,128)S(1)} fusion(f32[2048,1024]{1,0:T(8,128)} %param.12, f32[2048,64]{0,1:T(8,128)S(1)} %all_gather.6, f32[1024,64]{0,1:T(8,128)S(1)} %all_gather.7), kind=kOutput, calls=%fused_computation.2 | convolution fusion | flops 1619001344 | bytes 17563648 | tf_op jit(solution)/shard_map/dot_general | solution.py:14
  53.0 3.4 copy-done
  56.4 7.8 %fusion.25 = f32[2048,64]{1,0:T(8,128)} fusion(f32[2048,1024]{1,0:T(8,128)S(1)} %fusion, f32[1024,64]{0,1:T(8,128)S(1)} %all_gather.7), kind=kOutput, calls=%fused_computation.60 | convolution fusion | flops 1610612736 | bytes 9175040 | tf_op jit(solution)/shard_map/dot_general | solution.py:72
  65.0 69.3 %psum.56 = f32[64,64]{0,1:T(8,128)S(1)} all-reduce(f32[64,64]{0,1:T(8,128)S(1)} %fusion.24), channel_id=1, replica_groups=mesh['chan'=8,'tm'=16] {'chan','tm'}, use_global_device_ids=true, to_apply=%region_0.1 | all-reduce | flops 4096 | bytes 32768 | tf_op jit(solution)/shard_map/psum | solution.py:45
  134.4 5.8 %cholesky.74 = f32[64,64]{1,0:T(8,128)S(1)} custom-call(f32[64,64]{1,0:T(8,128)S(1)} %fusion.16), custom_call_target="Cholesky" | custom-call | tf_op jit(solution)/shard_map/jit(cholesky)/cholesky | solution.py:34
  141.6 4.9 custom-call.19
  146.5 6.8 %all-reduce.5.cloned.1.call-done = f32[2048,64]{1,0:T(8,128)} async-done(((f32[2048,64]{1,0:T(8,128)}), f32[2048,64]{1,0:T(8,128)}) %all-reduce.5.cloned.1.call-update) | async-done | bytes 524304 | tf_op jit(solution)/shard_map/psum | solution.py:71
  156.3 16.2 %fusion.26 = f32[1024,64]{1,0:T(8,128)} fusion(f32[2048,1024]{1,0:T(8,128)} %copy-done, f32[2048,64]{0,1:T(8,128)S(1)} %convolution_bitcast_fusion.1), kind=kOutput, calls=%fused_computation.61 | convolution fusion | flops 1610612736 | bytes 9175040 | tf_op jit(solution)/shard_map/dot_general | solution.py:24
  172.8 65.5 %psum.58 = f32[64,64]{0,1:T(8,128)S(1)} all-reduce(f32[64,64]{0,1:T(8,128)S(1)} %fusion.19), channel_id=1, replica_groups=mesh['chan'=8,'tm'=16] {'chan','tm'}, use_global_device_ids=true, to_apply=%region_4.8 | all-reduce | flops 4096 | bytes 32768 | tf_op jit(solution)/shard_map/psum | solution.py:45
  238.5 5.8 %cholesky.85 = f32[64,64]{1,0:T(8,128)S(1)} custom-call(f32[64,64]{1,0:T(8,128)S(1)} %fusion.13), custom_call_target="Cholesky" | custom-call | tf_op jit(solution)/shard_map/jit(cholesky)/cholesky | solution.py:34
  245.7 4.9 custom-call.21
  252.7 13.3 %fusion.23 = (f32[2048,1024]{1,0:T(8,128)}, f32[2048,1024]{1,0:T(8,128)}) fusion(f32[2048,1024]{1,0:T(8,128)} %param.12, f32[2048,64]{0,1:T(8,128)S(1)} %convolution_bitcast_fusion.1, f32[1024,64]{0,1:T(8,128)S(1)} %convolution_bitcast_fusion.7), kind=kOutput, calls=%fused_computation.58 | convolution fusion | flops 1619001344 | bytes 25952256 | tf_op jit(solution)/shard_map/dot_general | solution.py:14
  266.2 63.3 %psum.60 = f32[64,64]{0,1:T(8,128)S(1)} all-reduce(f32[64,64]{0,1:T(8,128)S(1)} %fusion.17), channel_id=1, replica_groups=mesh['chan'=8,'tm'=16] {'chan','tm'}, use_global_device_ids=true, to_apply=%region_6.12 | all-reduce | flops 4096 | bytes 32768 | tf_op jit(solution)/shard_map/psum | solution.py:45
  329.6 9.8 %fusion.27 = f32[2048,64]{1,0:T(8,128)} fusion(f32[2048,1024]{1,0:T(8,128)} %get-tuple-element.6, f32[1024,64]{0,1:T(8,128)S(1)} %convolution_bitcast_fusion.7), kind=kOutput, calls=%fused_computation.62 | convolution fusion | flops 1610612736 | bytes 9175040 | tf_op jit(solution)/shard_map/dot_general | solution.py:72
  339.7 5.8 %cholesky.96 = f32[64,64]{1,0:T(8,128)S(1)} custom-call(f32[64,64]{1,0:T(8,128)S(1)} %fusion.10), custom_call_target="Cholesky" | custom-call | tf_op jit(solution)/shard_map/jit(cholesky)/cholesky | solution.py:34
  346.9 4.9 custom-call.23
  351.8 70.1 %all-reduce.9.cloned.1.call-done = f32[2048,64]{1,0:T(8,128)} async-done(((f32[2048,64]{1,0:T(8,128)}), f32[2048,64]{1,0:T(8,128)}) %all-reduce.9.cloned.1.call-update) | async-done | bytes 524304 | tf_op jit(solution)/shard_map/psum | solution.py:71
  421.9 2.5 convolution_bitcast_fusion.2
  425.0 16.2 %fusion.29 = f32[1024,64]{1,0:T(8,128)} fusion(f32[2048,1024]{1,0:T(8,128)} %get-tuple-element.6, f32[2048,64]{0,1:T(8,128)S(1)} %convolution_bitcast_fusion), kind=kOutput, calls=%fused_computation.64 | convolution fusion | flops 1610612736 | bytes 9175040 | tf_op jit(solution)/shard_map/dot_general | solution.py:24
  441.4 66.3 %psum.62 = f32[64,64]{0,1:T(8,128)S(1)} all-reduce(f32[64,64]{0,1:T(8,128)S(1)} %fusion.28), channel_id=1, replica_groups=mesh['chan'=8,'tm'=16] {'chan','tm'}, use_global_device_ids=true, to_apply=%region_8.14 | all-reduce | flops 4096 | bytes 32768 | tf_op jit(solution)/shard_map/psum | solution.py:45
  507.9 5.8 %cholesky.107 = f32[64,64]{1,0:T(8,128)S(1)} custom-call(f32[64,64]{1,0:T(8,128)S(1)} %fusion.7), custom_call_target="Cholesky" | custom-call | tf_op jit(solution)/shard_map/jit(cholesky)/cholesky | solution.py:34
  515.1 4.9 custom-call.25
  (52 shorter events, 16.0 us)
Async XLA Ops:
  7.2 146.1 %all-reduce.5.cloned.1.call-start = ((), (), s32[]{:S(2)}) async-start(), calls=%async_computation | async-start | bytes 2097152 | tf_op jit(solution)/shard_map/psum | solution.py:71
  53.0 3.4 copy-start
  56.4 8.4 %copy-start.1 = (f32[128,64]{0,1:T(8,128)S(1)}, f32[128,64]{0,1:T(8,128)}, u32[]{:S(2)}) copy-start(f32[128,64]{0,1:T(8,128)} %param.14) | copy-start | bytes 98308
  64.2 186.4 %all-reduce.7.cloned.1.call-start = ((), (), s32[]{:S(2)}) async-start(), calls=%async_computation.1 | async-start | bytes 1048576 | tf_op jit(solution)/shard_map/psum | solution.py:85
  172.6 249.3 %all-reduce.9.cloned.1.call-start = ((), (), s32[]{:S(2)}) async-start(), calls=%async_computation.2 | async-start | bytes 2097152 | tf_op jit(solution)/shard_map/psum | solution.py:71
  339.4 180.6 %all-reduce.11.cloned.1.call-start = ((), (), s32[]{:S(2)}) async-start(), calls=%async_computation.3 | async-start | bytes 1048576 | tf_op jit(solution)/shard_map/psum | solution.py:85
  441.2 81.5 %copy-start.2 = (f32[128,64]{0,1:T(8,128)}, f32[128,64]{0,1:T(8,128)S(1)}, u32[]{:S(2)}) copy-start(f32[128,64]{0,1:T(8,128)S(1)} %constant_dynamic-slice_fusion.1) | copy-start | bytes 98308
Sparse Core Ops, SparseCore 0:
  64.3 88.8 all-reduce.4
  172.7 59.5 all-reduce.6
  339.5 82.3 all-reduce.8
  441.4 59.2 all-reduce.10
where the time goes:
time: 539 us; the launch traced here: 530 us
  blocking collectives  300 us (56%)
  matrix products  84.3 us (16%)
  waiting for transfers between devices  77 us (14%)
  other arithmetic  48.4 us (9%)
  between operations  14.4 us (3%)
    psum x4, blocking collectives, gram_sum(): return lax.psum(local_gram, ('chan', 'tm')) + ridge_weight * identity  264 us
    psum x2, waiting for transfers between devices, shards(): lax.psum(jnp.dot(cleaned, right_block, precision=lax.Precision.HIGHEST, p...  76.9 us
    dot_general x6, matrix products, cols_product(): lax.dot_general(first, second, (((0,), (0,)), ((), ())), precision=lax.Pr...  33.2 us
    another operation x12, other arithmetic, solve_ridge(): factor_chol = jnp.linalg.cholesky(gram)  26.1 us
    dot_general x2, matrix products, rows_product(): lax.dot_general(first, second, (((1,), (1,)), ((), ())), precision=lax.Pr...  23.2 us
    another operation x8, other arithmetic, solve_ridge(): lax.linalg.triangular_solve(factor_chol, middle, left_side=False, lower=T...  22.2 us
    all_gather x1, blocking collectives, gather_left(): return lax.all_gather(piece, 'tm', axis=0, tiled=True)  21 us
    dot_general x2, matrix products, shards(): jnp.dot(cleaned, right_block, precision=lax.Precision.HIGHEST, preferred_...  17.6 us
  transfers between devices with their start and end apart: 4, of which 2 were waited for; matrix products, arithmetic and copies ran while one was open for 9% of the time, Pallas kernels for 0%

commit v1 on v0

v1 whole, which is shorter than its diff:
```python
import functools

import jax
import jax.numpy as jnp
from jax import lax
from jax.experimental import pallas as pl
from jax.experimental.pallas import tpu as pltpu
from jax.sharding import PartitionSpec as P

THRESHOLD = 1.5
RIDGE = 8.0
RANK = 64
PIECE = 128
F32 = jnp.float32
BF16 = jnp.bfloat16
AXES = ("chan", "tm")
MIB = 1 << 20


def exact(first, second, dims):
    return lax.dot_general(
        first,
        second,
        (dims, ((), ())),
        precision=lax.Precision.HIGHEST,
        preferred_element_type=F32,
    )


def single(first, second, dims):
    return lax.dot_general(first, second, (dims, ((), ())), preferred_element_type=F32)


def low_lanes(shape):
    return lax.broadcasted_iota(jnp.int32, shape, 1) < RANK


def two_parts(values):
    high = values.astype(BF16)
    return high, (values - high.astype(F32)).astype(BF16)


def row_stack(packed):
    low = low_lanes(packed.shape)
    high = packed.astype(BF16).astype(F32)
    rest = packed - high
    first = jnp.where(low, high, pltpu.roll(rest, RANK, 1))
    second = jnp.where(low, pltpu.roll(high, RANK, 1), rest)
    return jnp.concatenate([first, second], axis=0).astype(BF16)


def pack_gram(gram):
    return jnp.concatenate([gram[:32], gram[32:]], axis=1)


def inverse(packed):
    flat = jnp.concatenate([packed, pltpu.roll(packed, RANK, 1)], axis=0)
    row = lax.broadcasted_iota(jnp.int32, (RANK, 2 * RANK), 0)
    lane = lax.broadcasted_iota(jnp.int32, (RANK, 2 * RANK), 1)
    flat = jnp.where(lane < RANK, flat, 0.0)
    flat = flat + jnp.where(lane == row, RIDGE, 0.0)
    flat = flat + jnp.where(lane == row + RANK, 1.0, 0.0)
    blocks = [flat[8 * b : 8 * b + 8] for b in range(8)]
    sub = lax.broadcasted_iota(jnp.int32, (8, 2 * RANK), 0)
    for k in range(RANK):
        b, s = divmod(k, 8)
        pivot_row = jnp.broadcast_to(blocks[b][s : s + 1], (8, 2 * RANK))
        pivot = jnp.broadcast_to(pivot_row[:, k : k + 1], (8, 2 * RANK))
        scaled = pivot_row / pivot
        for i in range(8):
            column = jnp.broadcast_to(blocks[i][:, k : k + 1], (8, 2 * RANK))
            changed = blocks[i] - column * scaled
            if i == b:
                changed = jnp.where(sub == s, scaled, changed)
            blocks[i] = changed
    return jnp.concatenate(blocks, axis=0)


def prep_kernel(chan_ref, time_ref, copies_ref, time_out):
    rows = chan_ref[...]
    packed = jnp.concatenate([rows[:RANK], rows[RANK:]], axis=1)
    for i in range(16):
        copies_ref[i] = packed
    time_out[...] = time_ref[...].T


def right_kernel(start, place_ref, *refs):
    if start:
        sources = refs[:4]
        wide_ref, tall_ref, gram_ref, held = refs[4:]
    else:
        mine_ref, other_ref, inv_ref = refs[:3]
        wide_ref, tall_ref, gram_ref, held = refs[3:]
    y, core = place_ref[0], place_ref[1]
    for k in range(4):
        spot = lax.rem(y + 4 - k, 4) if start else k
        if start:
            own, other = sources[k][:RANK], sources[k][RANK:]
        else:
            own, other = mine_ref[RANK * k : RANK * (k + 1)], other_ref[RANK * k : RANK * (k + 1)]
        held[2 * spot + core] = own
        held[2 * spot + 1 - core] = other
    full = jnp.concatenate([held[c] for c in range(8)], axis=1)
    if not start:
        full = exact(inv_ref[:RANK, :RANK], full, ((1,), (0,)))
    gram_ref[...] = pack_gram(exact(full, full, ((1,), (1,))))
    high, low = two_parts(full)
    wide_ref[0:64] = high
    wide_ref[64:128] = high
    wide_ref[128:192] = low
    wide_ref[192:256] = low
    tall_ref[0:64] = high
    tall_ref[64:128] = low


def piece_of(core, q, i):
    return jnp.where(core == 0, 4 * q + i, 4 * i + q)


def rows_kernel(start, j, place_ref, a_ref, left_ref, wide_ref, tall_ref, gram_ref, s_ref, h_ref, l_ref):
    core, u = place_ref[1], place_ref[2]
    q = lax.rem(u + j + 1, 4)
    low = low_lanes((RANK, PIECE))
    for half in range(2):
        spots = []
        stacks = []
        for i in (2 * half, 2 * half + 1):
            p = piece_of(core, q, i)
            spots.append(pl.multiple_of(p * PIECE, PIECE))
            packed = left_ref[p] if start else left_ref[RANK * i : RANK * (i + 1)]
            stacks.append(row_stack(packed))
        stack = jnp.concatenate(stacks, axis=0)
        stack = jnp.concatenate([stack, stack], axis=1)
        total = jnp.zeros((256, PIECE), F32)
        for t in range(4):
            cols = slice(256 * t, 256 * t + 256)
            product = single(stack, wide_ref[:, cols], ((1,), (0,)))
            values = jnp.concatenate([a_ref[pl.ds(s, PIECE), cols] for s in spots], axis=0)
            cleaned = product + jnp.clip(values - product, -THRESHOLD, THRESHOLD)
            high, rest = two_parts(cleaned)
            for n in range(2):
                i = 2 * half + n
                for part, ref in ((high, h_ref), (rest, l_ref)):
                    ref[64 * i : 64 * i + 64, cols] = part[128 * n : 128 * n + 64]
                    ref[256 + 64 * i : 320 + 64 * i, cols] = part[128 * n + 64 : 128 * n + 128]
            total += single(high, tall_ref[:, cols], ((1,), (1,)))
            total += single(rest, tall_ref[:, cols], ((1,), (1,)))
        total = total + pltpu.roll(total, RANK, 1)
        for n in range(2):
            i = 2 * half + n
            s_ref[64 * i : 64 * i + 64] = jnp.where(low, total[128 * n : 128 * n + 64], total[128 * n + 64 : 128 * n + 128])
    s_ref[256:288] = gram_ref[...]


def inverse_kernel(sum_ref, inv_ref):
    found = inverse(sum_ref[256:288])
    low = low_lanes((RANK, PIECE))
    inv_ref[0:64] = jnp.where(low, pltpu.roll(found, RANK, 1), 0.0)
    inv_ref[64:128] = jnp.where(low, 0.0, found)


def cols_kernel(count, has_acc, last, place_ref, inv_ref, *refs):
    s_refs, h_refs, l_refs = refs[:count], refs[count : 2 * count], refs[2 * count : 3 * count]
    refs = refs[3 * count :]
    if has_acc:
        acc_ref, acc_gram_ref = refs[:2]
        refs = refs[2:]
        mine_ref, other_ref = refs[:2]
    else:
        t_ref, gram_ref = refs[:2]
    left_refs = refs[2:]
    core, v = place_ref[1], place_ref[3]
    inv = inv_ref[...]
    gram = acc_gram_ref[...] if has_acc else jnp.zeros((RANK, RANK), F32)
    stacks = []
    for k in range(count):
        packed = exact(s_refs[k][0:256], inv, ((1,), (0,)))
        if not last:
            left_refs[k][...] = packed
        elif not has_acc:
            held = left_refs[1]
            held[...] = packed
            own = held[pl.ds(pl.multiple_of(v * RANK, RANK), RANK)]
            left_refs[0][...] = jnp.concatenate([own[:, :RANK], own[:, RANK:]], axis=0)
        turned = packed.T
        turned = jnp.concatenate([turned[:RANK], turned[RANK:]], axis=1)
        gram += exact(turned, turned, ((1,), (1,)))
        high, rest = two_parts(turned)
        stacks.append(jnp.concatenate([high, rest], axis=0))
    tiles = []
    for t in range(4):
        cols = slice(256 * t, 256 * t + 256)
        total = jnp.zeros((PIECE, 256), F32)
        for k in range(count):
            total += single(stacks[k], h_refs[k][:, cols], ((1,), (0,)))
            total += single(stacks[k], l_refs[k][:, cols], ((1,), (0,)))
        part = total[:RANK] + total[RANK:]
        if has_acc:
            part += acc_ref[:, cols]
            even, odd = part[:, :PIECE], part[:, PIECE:]
            mine_ref[RANK * t : RANK * (t + 1)] = jnp.where(core == 0, even, odd)
            other_ref[RANK * t : RANK * (t + 1)] = jnp.where(core == 0, odd, even)
        else:
            t_ref[:, cols] = part
    if has_acc:
        mine_ref[256:288] = pack_gram(gram)
        other_ref[256:288] = pack_gram(gram)
    else:
        gram_ref[...] = gram


def message_kernel(place_ref, first_ref, second_ref, *out_refs):
    y = place_ref[0]
    gram = first_ref[256:288] + second_ref[256:288]
    for k in range(4):
        rows = pl.ds(pl.multiple_of(lax.rem(y + k, 4) * RANK, RANK), RANK)
        out_refs[k][0:64] = first_ref[rows] + second_ref[rows]
        out_refs[k][64:96] = gram


def final_kernel(m0, m1, m2, m3, out_ref):
    total = m0[...] + m1[...] + m2[...] + m3[...]
    found = inverse(total[64:96])[:, RANK:]
    out_ref[...] = exact(found, total[:64], ((1,), (0,))).T


def outlier_kernel(spots_ref, left_ref, wide_ref, a_ref, out_ref):
    g = pl.program_id(0)
    stack = row_stack(left_ref[pl.ds(pl.multiple_of(g * RANK, RANK), RANK)])
    stack = jnp.concatenate([stack, stack], axis=1)
    for t in range(4):
        cols = slice(256 * t, 256 * t + 256)
        residue = a_ref[:, cols] - single(stack, wide_ref[:, cols], ((1,), (0,)))
        out_ref[:, cols] = residue - jnp.clip(residue, -THRESHOLD, THRESHOLD)


VM = pl.BlockSpec(memory_space=pltpu.VMEM)
SM = pl.BlockSpec(memory_space=pltpu.SMEM)


def shape(*dims, dtype=F32):
    return jax.ShapeDtypeStruct(dims, dtype)


def call(kernel, outs, args, scratch=(), name=None, flops=0, limit=16):
    return pl.pallas_call(
        kernel,
        out_shape=outs,
        in_specs=[SM if a.dtype == jnp.int32 else VM for a in args],
        out_specs=[VM for _ in outs],
        scratch_shapes=list(scratch),
        compiler_params=pltpu.CompilerParams(vmem_limit_bytes=limit * MIB),
        cost_estimate=pl.CostEstimate(flops=flops, bytes_accessed=MIB, transcendentals=0),
        name=name,
    )(*args)


def ring(kind, k):
    pairs = []
    for chan in range(8):
        for tm in range(16):
            y, core = divmod(chan, 2)
            x, z = divmod(tm, 4)
            axis = kind
            if kind == "u":
                axis = "xz"[core]
            elif kind == "v":
                axis = "zx"[core]
            if axis == "x":
                x = (x + k) % 4
            elif axis == "z":
                z = (z + k) % 4
            elif axis == "y":
                y = (y + k) % 4
            else:
                core = 1 - core
            pairs.append((chan * 16 + tm, (2 * y + core) * 16 + 4 * x + z))
    return pairs


def send(values, kind, k=1):
    return lax.ppermute(values, AXES, ring(kind, k))


def sum_around(values, kind):
    return values + send(values, kind, 1) + send(values, kind, 2) + send(values, kind, 3)


def shards(readings, channel_start, time_start):
    chan, tm = lax.axis_index("chan"), lax.axis_index("tm")
    y, core, x, z = chan // 2, chan % 2, tm // 4, tm % 4
    u, v = jnp.where(core == 0, x, z), jnp.where(core == 0, z, x)
    place = jnp.stack([y, core, u, v]).astype(jnp.int32)
    values = readings

    copies, time_piece = call(prep_kernel, [shape(16, 64, 128), shape(64, 128)], [channel_start, time_start], name="prep")
    pair = jnp.concatenate([time_piece, send(time_piece, "core")], axis=0)
    around = [pair] + [send(pair, "y", k) for k in (1, 2, 3)]
    lefts = lax.all_to_all(copies, "tm", split_axis=0, concat_axis=0, tiled=True)
    lefts = [lefts] * 4

    right_args = around
    for sweep in range(2):
        start, last = sweep == 0, sweep == 1
        wide, tall, gram = call(
            functools.partial(right_kernel, start),
            [shape(256, 1024, dtype=BF16), shape(128, 1024, dtype=BF16), shape(32, 128)],
            [place] + list(right_args),
            scratch=[pltpu.VMEM((8, 64, 128), F32)],
            name="right",
        )
        sums, highs, rests = [], [], []
        for j in range(4):
            s, h, r = call(
                functools.partial(rows_kernel, start, j),
                [shape(288, 128), shape(512, 1024, dtype=BF16), shape(512, 1024, dtype=BF16)],
                [place, values, lefts[3 - j], wide, tall, gram],
                name="rows",
                flops=2 * 512 * 1024 * 768,
            )
            sums.append(s)
            highs.append(h)
            rests.append(r)
        got = [send(sums[k - 1], "u", k) for k in (1, 2, 3)]
        own = sums[3] + got[0] + got[1] + got[2]
        own = sum_around(own, "v")
        (inv,) = call(inverse_kernel, [shape(128, 128)], [own], name="inverse", flops=10**9)
        quarters = [own] + [send(own, "u", k) for k in (1, 2, 3)]
        if last:
            left_all = jnp.concatenate(lefts, axis=0)
        first_outs = [shape(64, 1024), shape(64, 64)]
        first_scratch = []
        if last:
            first_outs.append(shape(128, 64))
            first_scratch.append(pltpu.VMEM((256, 128), F32))
        else:
            first_outs.append(shape(256, 128))
        acc, acc_gram, first_left = call(
            functools.partial(cols_kernel, 1, False, last),
            first_outs,
            [place, inv, own, highs[3], rests[3]],
            scratch=first_scratch,
            name="cols_own",
            flops=2 * 512 * 1024 * 256,
        )
        order = (2, 1, 0)
        outs = [shape(288, 128), shape(288, 128)] + ([] if last else [shape(256, 128)] * 3)
        mine, other, *more = call(
            functools.partial(cols_kernel, 3, True, last),
            outs,
            [place, inv] + quarters[1:] + [highs[i] for i in order] + [rests[i] for i in order] + [acc, acc_gram],
            name="cols_rest",
            flops=2 * 1536 * 1024 * 256,
        )
        swapped = send(other, "core")
        if not last:
            half = sum_around(mine + swapped, "y")
            (inv,) = call(inverse_kernel, [shape(128, 128)], [half], name="inverse", flops=10**9)
            right_args = [half, send(half, "core"), inv]
            lefts = [first_left] + list(more)
    messages = call(message_kernel, [shape(96, 128)] * 4, [place, mine, swapped], name="messages")
    parts = [messages[0]] + [send(messages[k], "y", k) for k in (1, 2, 3)]
    (time_out,) = call(final_kernel, [shape(128, 64)], parts, name="final")

    q = jnp.stack([(u + 4 - g // 4) % 4 for g in range(16)])
    i = jnp.arange(16) % 4
    spots = jnp.where(core == 0, 4 * q + i, 4 * i + q).astype(jnp.int32)
    outliers = pl.pallas_call(
        outlier_kernel,
        out_shape=shape(2048, 1024),
        grid_spec=pltpu.PrefetchScalarGridSpec(
            num_scalar_prefetch=1,
            grid=(16,),
            in_specs=[
                pl.BlockSpec((1024, 128), lambda g, spots: (0, 0)),
                pl.BlockSpec((256, 1024), lambda g, spots: (0, 0)),
                pl.BlockSpec((128, 1024), lambda g, spots: (spots[g], 0)),
            ],
            out_specs=pl.BlockSpec((128, 1024), lambda g, spots: (spots[g], 0)),
        ),
        compiler_params=pltpu.CompilerParams(vmem_limit_bytes=16 * MIB),
        cost_estimate=pl.CostEstimate(flops=2 * 2048 * 1024 * 256, bytes_accessed=16 * MIB, transcendentals=0),
        name="outliers",
    )(spots, left_all, wide, readings)
    return outliers, first_left, time_out


def solution(mesh):
    in_specs = (P("chan", "tm"), P(("chan", "tm"), None), P(("tm", "chan"), None))
    out_specs = (P("chan", "tm"), P(("chan", "tm"), None), P(("tm", "chan"), None))
    return jax.shard_map(shards, mesh=mesh, in_specs=in_specs, out_specs=out_specs, check_vma=False)
```

time: 539 us -> 175 us (0.32); the launches traced: 530 us -> 174 us
  blocking collectives: 300 us -> 0 us
  matrix products: 84.3 us -> 0 us
  Pallas kernels: 0 us -> 72.9 us
  waiting for transfers between devices: 77 us -> 18.8 us
  starting transfers between devices: 0.9 us -> 58 us
  other arithmetic: 48.4 us -> 0.33 us
  local copies, waits for them, and re-layouts: 4.33 us -> 23.2 us
  between operations: 14.4 us -> 0.99 us
    psum x4 -> x0, blocking collectives: 264 us -> none  [gram_sum(): return lax.psum(local_gram, ('chan', 'tm')) + ridge_weight * identity]
    psum x4 -> x0, waiting for transfers between devices: 77 us -> none  [the longest x2 76.9 us: shards(): lax.psum(jnp.dot(cleaned, right_block, precision=lax.Precision.HIGHEST, p...]
    dot_general x10 -> x0, matrix products: 73.9 us -> none  [the longest x6 33.2 us: cols_product(): lax.dot_general(first, second, (((0,), (0,)), ((), ())), precision=lax.Pr...]
    pallas_call x0 -> x21, Pallas kernels: none -> 72.9 us  [the longest x20 63.5 us: call(): pl.pallas_call(kernel, out_shape=outs, in_specs=[SM if a.dtype == jnp.int...]
    ppermute x0 -> x31, starting transfers between devices: none -> 49.5 us  [send(): return lax.ppermute(values, AXES, ring(kind, k))]
    another operation x20 -> x1, other arithmetic: 48.3 us -> 0.08 us  [shards(): place = jnp.stack([y, core, u, v]).astype(jnp.int32)]
    all_gather x2 -> x0, blocking collectives: 35.9 us -> none  [the longest x1 21 us: gather_left(): return lax.all_gather(piece, 'tm', axis=0, tiled=True)]
    unnamed x6 -> x37, local copies, waits for them, and re-layouts: 3.4 us -> 23.1 us
  transfers between devices with their start and end apart: 4 -> 32, of which waited for: 2 -> 15; matrix products, arithmetic and copies ran while one was open for 9% -> 1% of each run, Pallas kernels for 0% -> 30%
where the time goes in v1:
time: 175 us; the launch traced here: 174 us
  Pallas kernels  72.9 us (42%)
  starting transfers between devices  58 us (33%)
  local copies, waits for them, and re-layouts  23.2 us (13%)
  waiting for transfers between devices  18.8 us (11%)
    pallas_call x20, Pallas kernels, call(): pl.pallas_call(kernel, out_shape=outs, in_specs=[SM if a.dtype == jnp.int...  63.5 us
    ppermute x31, starting transfers between devices, send(): return lax.ppermute(values, AXES, ring(kind, k))  49.5 us
    unnamed x37, local copies, waits for them, and re-layouts  23.1 us
    ppermute x31, waiting for transfers between devices, send(): return lax.ppermute(values, AXES, ring(kind, k))  18.7 us
    pallas_call x1, Pallas kernels, shards(): pl.pallas_call(outlier_kernel, out_shape=shape(2048, 1024), grid_spec=plt...  9.42 us
    all_to_all x1, starting transfers between devices, shards(): lax.all_to_all(copies, 'tm', split_axis=0, concat_axis=0, tiled=True)  8.43 us
  transfers between devices with their start and end apart: 32, of which 15 were waited for; matrix products, arithmetic and copies ran while one was open for 1% of the time, Pallas kernels for 30%

profile of v1, /device:TPU:1, one launch (start us, length us, event | category | flops | bytes accessed | tf_op | source)
XLA Modules:
  0.0 174.2 jit_solution(3194413042338947585)
XLA Ops:
  3.3 8.4 %all-to-all-start = ((f32[16,64,128]{2,1,0:T(8,128)}), f32[16,64,128]{2,1,0:T(8,128)S(1)}, u32[]{:S(2)}, u32[]{:S(2)}) async-start(f32[16,64,128]{2,1,0:T(8,128)} %get-tuple-element.52), calls=%async_computation | async-start | bytes 1048576 | tf_op jit(solution)/shard_map/all_to_all | solution.py:299
  14.9 2.6 %collective-permute-start.2 = (f32[128,128]{1,0:T(8,128)S(1)}, f32[128,128]{1,0:T(8,128)S(1)}, u32[]{:S(2)}, u32[]{:S(2)}) collective-permute-start(f32[128,128]{1,0:T(8,128)S(1)} %constant_dynamic-update-slice_fusion.refs_0_), channel_id=1, source_target_pairs={{0,64},{1,65},{2,66},{3,67},{4,68},{5,69},{6,70},{7,71},{8,72},{9,... | collective-permute-start | bytes 196616 | tf_op jit(solution)/shard_map/ppermute | solution.py:282
  18.7 2.1 %collective-permute-done.2.refs_2_ = f32[128,128]{1,0:T(8,128)S(1)} collective-permute-done((f32[128,128]{1,0:T(8,128)S(1)}, f32[128,128]{1,0:T(8,128)S(1)}, u32[]{:S(2)}, u32[]{:S(2)}) %collective-permute-start.2) | collective-permute-done | bytes 65568 | tf_op jit(solution)/shard_map/ppermute | solution.py:282
  22.0 3.4 %copy-done = f32[2048,1024]{1,0:T(8,128)S(1)} copy-done((f32[2048,1024]{1,0:T(8,128)S(1)}, f32[2048,1024]{1,0:T(8,128)}, u32[]{:S(2)}) %copy-start) | copy-done | bytes 8388632
  31.1 2.5 %collective-permute-start.5 = (f32[288,128]{1,0:T(8,128)S(1)}, f32[288,128]{1,0:T(8,128)S(1)}, u32[]{:S(2)}, u32[]{:S(2)}) collective-permute-start(f32[288,128]{1,0:T(8,128)S(1)} %get-tuple-element.59), channel_id=1, source_target_pairs={{0,8},{1,9},{2,10},{3,11},{4,12},{5,13},{6,14},{7,15},{8,0},{9,1},... | collective-permute-start | bytes 442376 | tf_op jit(solution)/shard_map/ppermute | solution.py:282
  45.1 2.5 %collective-permute-done.8 = f32[288,128]{1,0:T(8,128)S(1)} collective-permute-done((f32[288,128]{1,0:T(8,128)S(1)}, f32[288,128]{1,0:T(8,128)S(1)}, u32[]{:S(2)}, u32[]{:S(2)}) %collective-permute-start.8) | collective-permute-done | bytes 147488 | tf_op jit(solution)/shard_map/ppermute | solution.py:282
  47.9 3.6 %collective-permute-start.11 = (f32[288,128]{1,0:T(8,128)S(1)}, f32[288,128]{1,0:T(8,128)S(1)}, u32[]{:S(2)}, u32[]{:S(2)}) collective-permute-start(f32[288,128]{1,0:T(8,128)S(1)} %add_add_fusion.3.sum_ref.refs_0_), channel_id=1, source_target_pairs={{0,8},{1,9},{2,10},{3,11},{4,12},{5,13},{6,14},{7,15},{8,0},{9,1},... | collective-permute-start | bytes 442376 | tf_op jit(solution)/shard_map/ppermute | solution.py:282
  51.4 8.5 %inverse.3.inv_ref = f32[128,128]{1,0:T(8,128)S(1)} custom-call(f32[288,128]{1,0:T(8,128)S(1)} %add_add_fusion.3.sum_ref.refs_0_), custom_call_target="tpu_custom_call" | custom-call | flops 1000000000 | bytes 1048576 | tf_op jit(solution)/shard_map/inverse/pallas_call | solution.py:246
  61.6 2.5 %cols_rest.2 = (f32[288,128]{1,0:T(8,128)S(1)}, f32[288,128]{1,0:T(8,128)S(1)}, f32[256,128]{1,0:T(8,128)S(1)}, f32[256,128]{1,0:T(8,128)S(1)}, f32[256,128]{1,0:T(8,128)S(1)}) custom-call(s32[4]{0:T(128)S(1)} %pad_add_fusion.place_ref, f32[128,128]{1,0:T(8,128)S(1)} %inverse.3.inv_ref, f32[288,128]{1,0:T(8,128)S(1)} %collective-permute-done.10.refs_0_, ...), custom_call_target="tpu_custom_call" | custom-call | flops 805306368 | bytes 1048576 | tf_op jit(solution)/shard_map/cols_rest/pallas_call | solution.py:246
  64.1 5.5 %collective-permute-start.13 = (f32[288,128]{1,0:T(8,128)S(1)}, f32[288,128]{1,0:T(8,128)S(1)}, u32[]{:S(2)}, u32[]{:S(2)}) collective-permute-start(f32[288,128]{1,0:T(8,128)S(1)} %get-tuple-element.76), channel_id=1, source_target_pairs={{0,16},{1,17},{2,18},{3,19},{4,20},{5,21},{6,22},{7,23},{8,24},{9,... | collective-permute-start | bytes 442376 | tf_op jit(solution)/shard_map/ppermute | solution.py:282
  71.0 3.2 %collective-permute-start.15 = (f32[288,128]{1,0:T(8,128)S(1)}, f32[288,128]{1,0:T(8,128)S(1)}, u32[]{:S(2)}, u32[]{:S(2)}) collective-permute-start(f32[288,128]{1,0:T(8,128)S(1)} %add.138), channel_id=1, source_target_pairs={{0,64},{1,65},{2,66},{3,67},{4,68},{5,69},{6,70},{7,71},{8,72},{9,... | collective-permute-start | bytes 442376 | tf_op jit(solution)/shard_map/ppermute | solution.py:282
  74.3 2.7 %collective-permute-done.14 = f32[288,128]{1,0:T(8,128)S(1)} collective-permute-done((f32[288,128]{1,0:T(8,128)S(1)}, f32[288,128]{1,0:T(8,128)S(1)}, u32[]{:S(2)}, u32[]{:S(2)}) %collective-permute-start.14) | collective-permute-done | bytes 147488 | tf_op jit(solution)/shard_map/ppermute | solution.py:282
  77.0 3.9 %collective-permute-done.15 = f32[288,128]{1,0:T(8,128)S(1)} collective-permute-done((f32[288,128]{1,0:T(8,128)S(1)}, f32[288,128]{1,0:T(8,128)S(1)}, u32[]{:S(2)}, u32[]{:S(2)}) %collective-permute-start.15) | collective-permute-done | bytes 147488 | tf_op jit(solution)/shard_map/ppermute | solution.py:282
  82.3 8.5 %inverse.4.refs_2_ = f32[128,128]{1,0:T(8,128)S(1)} custom-call(f32[288,128]{1,0:T(8,128)S(1)} %add_add_fusion.2.sum_ref.refs_0_), custom_call_target="tpu_custom_call" | custom-call | flops 1000000000 | bytes 1048576 | tf_op jit(solution)/shard_map/inverse/pallas_call | solution.py:246
  94.4 2.8 %collective-permute-start.18 = (f32[288,128]{1,0:T(8,128)S(1)}, f32[288,128]{1,0:T(8,128)S(1)}, u32[]{:S(2)}, u32[]{:S(2)}) collective-permute-start(f32[288,128]{1,0:T(8,128)S(1)} %get-tuple-element.81), channel_id=1, source_target_pairs={{0,4},{1,5},{2,6},{3,7},{4,8},{5,9},{6,10},{7,11},{8,12},{9,13},{1... | collective-permute-start | bytes 442376 | tf_op jit(solution)/shard_map/ppermute | solution.py:282
  114.3 2.4 %collective-permute-start.23 = (f32[288,128]{1,0:T(8,128)S(1)}, f32[288,128]{1,0:T(8,128)S(1)}, u32[]{:S(2)}, u32[]{:S(2)}) collective-permute-start(f32[288,128]{1,0:T(8,128)S(1)} %add_add_fusion.1), channel_id=1, source_target_pairs={{0,3},{1,0},{2,1},{3,2},{4,7},{5,4},{6,5},{7,6},{8,11},{9,8},{10,9... | collective-permute-start | bytes 442376 | tf_op jit(solution)/shard_map/ppermute | solution.py:282
  117.6 2.3 %collective-permute-done.22 = f32[288,128]{1,0:T(8,128)S(1)} collective-permute-done((f32[288,128]{1,0:T(8,128)S(1)}, f32[288,128]{1,0:T(8,128)S(1)}, u32[]{:S(2)}, u32[]{:S(2)}) %collective-permute-start.22) | collective-permute-done | bytes 147488 | tf_op jit(solution)/shard_map/ppermute | solution.py:282
  123.0 8.5 %inverse.5.inv_ref = f32[128,128]{1,0:T(8,128)S(1)} custom-call(f32[288,128]{1,0:T(8,128)S(1)} %add_add_fusion.sum_ref.refs_0_), custom_call_target="tpu_custom_call" | custom-call | flops 1000000000 | bytes 1048576 | tf_op jit(solution)/shard_map/inverse/pallas_call | solution.py:246
  140.5 3.0 %cols_rest.3 = (f32[288,128]{1,0:T(8,128)S(1)}, f32[288,128]{1,0:T(8,128)S(1)}) custom-call(s32[4]{0:T(128)S(1)} %pad_add_fusion.place_ref, f32[128,128]{1,0:T(8,128)S(1)} %inverse.5.inv_ref, f32[288,128]{1,0:T(8,128)S(1)} %collective-permute-done.24.refs_0_, f32[288,128]{1,0:T(8,128)} %collective-permute-done.25.refs_1_, ...), custom_call_target="tpu_custom_call" | custom-call | flops 805306368 | bytes 1048576 | tf_op jit(solution)/shard_map/cols_rest/pallas_call | solution.py:246
  143.4 3.0 %collective-permute-start.27 = (f32[288,128]{1,0:T(8,128)S(1)}, f32[288,128]{1,0:T(8,128)S(1)}, u32[]{:S(2)}, u32[]{:S(2)}) collective-permute-start(f32[288,128]{1,0:T(8,128)S(1)} %get-tuple-element.96), channel_id=1, source_target_pairs={{0,16},{1,17},{2,18},{3,19},{4,20},{5,21},{6,22},{7,23},{8,24},{9,... | collective-permute-start | bytes 442376 | tf_op jit(solution)/shard_map/ppermute | solution.py:282
  148.4 2.8 %collective-permute-start.29 = (f32[96,128]{1,0:T(8,128)S(1)}, f32[96,128]{1,0:T(8,128)S(1)}, u32[]{:S(2)}, u32[]{:S(2)}) collective-permute-start(f32[96,128]{1,0:T(8,128)S(1)} %get-tuple-element.99), channel_id=1, source_target_pairs={{0,64},{1,65},{2,66},{3,67},{4,68},{5,69},{6,70},{7,71},{8,72},{9,... | collective-permute-start | bytes 147464 | tf_op jit(solution)/shard_map/ppermute | solution.py:282
  151.2 3.4 %copy-done.1 = f32[2048,1024]{1,0:T(8,128)S(1)} copy-done((f32[2048,1024]{1,0:T(8,128)S(1)}, f32[2048,1024]{1,0:T(8,128)}, u32[]{:S(2)}) %copy-start.1) | copy-done | bytes 8388632
  154.6 9.4 %outliers.1 = f32[2048,1024]{1,0:T(8,128)} custom-call(s32[16]{0:T(128)S(1)} %broadcast_select_fusion.spots_ref, f32[1024,128]{1,0:T(8,128)S(1)} %pad_maximum_fusion.left_ref, bf16[256,1024]{1,0:T(8,128)(2,1)S(1)} %get-tuple-element.77.wide_ref, f32[2048,1024]{1,0:T(8,128)S(1)} %copy-done.1), custom_call_target="tpu_custom_call" | custom-call | flops 1073741824 | bytes 16777216 | tf_op jit(solution)/shard_map/outliers/pallas_call | solution.py:368
  164.7 8.8 %final.1 = f32[128,64]{1,0:T(8,128)S(1)} custom-call(f32[96,128]{1,0:T(8,128)S(1)} %get-tuple-element.97.m0, f32[96,128]{1,0:T(8,128)S(1)} %collective-permute-done.28.m1, f32[96,128]{1,0:T(8,128)S(1)} %collective-permute-done.29.m2, f32[96,128]{1,0:T(8,128)S(1)} %collective-permute-done.30.m3), custom_call_target="tpu_custom_call" | custom-call | bytes 1048576 | tf_op jit(solution)/shard_map/final/pallas_call | solution.py:246
  (110 shorter events, 66.7 us)
Async XLA Ops:
  3.3 18.7 %all-to-all-start = ((f32[16,64,128]{2,1,0:T(8,128)}), f32[16,64,128]{2,1,0:T(8,128)S(1)}, u32[]{:S(2)}, u32[]{:S(2)}) async-start(f32[16,64,128]{2,1,0:T(8,128)} %get-tuple-element.52), calls=%async_computation | async-start | bytes 1048576 | tf_op jit(solution)/shard_map/all_to_all | solution.py:299
  14.9 5.9 %collective-permute-start.2 = (f32[128,128]{1,0:T(8,128)S(1)}, f32[128,128]{1,0:T(8,128)S(1)}, u32[]{:S(2)}, u32[]{:S(2)}) collective-permute-start(f32[128,128]{1,0:T(8,128)S(1)} %constant_dynamic-update-slice_fusion.refs_0_), channel_id=1, source_target_pairs={{0,64},{1,65},{2,66},{3,67},{4,68},{5,69},{6,70},{7,71},{8,72},{9,... | collective-permute-start | bytes 196616 | tf_op jit(solution)/shard_map/ppermute | solution.py:282
  27.5 11.6 %collective-permute-start.4 = (f32[288,128]{1,0:T(8,128)S(1)}, f32[288,128]{1,0:T(8,128)S(1)}, u32[]{:S(2)}, u32[]{:S(2)}) collective-permute-start(f32[288,128]{1,0:T(8,128)S(1)} %get-tuple-element.58), channel_id=1, source_target_pairs={{0,4},{1,5},{2,6},{3,7},{4,8},{5,9},{6,10},{7,11},{8,12},{9,13},{1... | collective-permute-start | bytes 442376 | tf_op jit(solution)/shard_map/ppermute | solution.py:282
  31.1 7.9 %collective-permute-start.5 = (f32[288,128]{1,0:T(8,128)S(1)}, f32[288,128]{1,0:T(8,128)S(1)}, u32[]{:S(2)}, u32[]{:S(2)}) collective-permute-start(f32[288,128]{1,0:T(8,128)S(1)} %get-tuple-element.59), channel_id=1, source_target_pairs={{0,8},{1,9},{2,10},{3,11},{4,12},{5,13},{6,14},{7,15},{8,0},{9,1},... | collective-permute-start | bytes 442376 | tf_op jit(solution)/shard_map/ppermute | solution.py:282
  41.4 6.2 %collective-permute-start.8 = (f32[288,128]{1,0:T(8,128)S(1)}, f32[288,128]{1,0:T(8,128)S(1)}, u32[]{:S(2)}, u32[]{:S(2)}) collective-permute-start(f32[288,128]{1,0:T(8,128)S(1)} %add_add_fusion.4), channel_id=1, source_target_pairs={{0,2},{1,3},{2,0},{3,1},{4,6},{5,7},{6,4},{7,5},{8,10},{9,11},{10,... | collective-permute-start | bytes 442376 | tf_op jit(solution)/shard_map/ppermute | solution.py:282
  47.8 13.7 %collective-permute-start.10 = (f32[288,128]{1,0:T(8,128)S(1)}, f32[288,128]{1,0:T(8,128)S(1)}, u32[]{:S(2)}, u32[]{:S(2)}) collective-permute-start(f32[288,128]{1,0:T(8,128)S(1)} %add_add_fusion.3.sum_ref.refs_0_), channel_id=1, source_target_pairs={{0,4},{1,5},{2,6},{3,7},{4,8},{5,9},{6,10},{7,11},{8,12},{9,13},{1... | collective-permute-start | bytes 442376 | tf_op jit(solution)/shard_map/ppermute | solution.py:282
  47.9 13.7 %collective-permute-start.11 = (f32[288,128]{1,0:T(8,128)S(1)}, f32[288,128]{1,0:T(8,128)S(1)}, u32[]{:S(2)}, u32[]{:S(2)}) collective-permute-start(f32[288,128]{1,0:T(8,128)S(1)} %add_add_fusion.3.sum_ref.refs_0_), channel_id=1, source_target_pairs={{0,8},{1,9},{2,10},{3,11},{4,12},{5,13},{6,14},{7,15},{8,0},{9,1},... | collective-permute-start | bytes 442376 | tf_op jit(solution)/shard_map/ppermute | solution.py:282
  51.4 10.1 %collective-permute-start.12 = (f32[288,128]{1,0:T(8,128)S(1)}, f32[288,128]{1,0:T(8,128)S(1)}, u32[]{:S(2)}, u32[]{:S(2)}) collective-permute-start(f32[288,128]{1,0:T(8,128)S(1)} %add_add_fusion.3.sum_ref.refs_0_), channel_id=1, source_target_pairs={{0,12},{1,13},{2,14},{3,15},{4,0},{5,1},{6,2},{7,3},{8,4},{9,5},{1... | collective-permute-start | bytes 442376 | tf_op jit(solution)/shard_map/ppermute | solution.py:282
  64.1 6.5 %collective-permute-start.13 = (f32[288,128]{1,0:T(8,128)S(1)}, f32[288,128]{1,0:T(8,128)S(1)}, u32[]{:S(2)}, u32[]{:S(2)}) collective-permute-start(f32[288,128]{1,0:T(8,128)S(1)} %get-tuple-element.76), channel_id=1, source_target_pairs={{0,16},{1,17},{2,18},{3,19},{4,20},{5,21},{6,22},{7,23},{8,24},{9,... | collective-permute-start | bytes 442376 | tf_op jit(solution)/shard_map/ppermute | solution.py:282
  70.7 6.3 %collective-permute-start.14 = (f32[288,128]{1,0:T(8,128)S(1)}, f32[288,128]{1,0:T(8,128)S(1)}, u32[]{:S(2)}, u32[]{:S(2)}) collective-permute-start(f32[288,128]{1,0:T(8,128)S(1)} %add.138), channel_id=1, source_target_pairs={{0,32},{1,33},{2,34},{3,35},{4,36},{5,37},{6,38},{7,39},{8,40},{9,... | collective-permute-start | bytes 442376 | tf_op jit(solution)/shard_map/ppermute | solution.py:282
  71.0 10.0 %collective-permute-start.15 = (f32[288,128]{1,0:T(8,128)S(1)}, f32[288,128]{1,0:T(8,128)S(1)}, u32[]{:S(2)}, u32[]{:S(2)}) collective-permute-start(f32[288,128]{1,0:T(8,128)S(1)} %add.138), channel_id=1, source_target_pairs={{0,64},{1,65},{2,66},{3,67},{4,68},{5,69},{6,70},{7,71},{8,72},{9,... | collective-permute-start | bytes 442376 | tf_op jit(solution)/shard_map/ppermute | solution.py:282
  74.2 6.8 %collective-permute-start.16 = (f32[288,128]{1,0:T(8,128)S(1)}, f32[288,128]{1,0:T(8,128)S(1)}, u32[]{:S(2)}, u32[]{:S(2)}) collective-permute-start(f32[288,128]{1,0:T(8,128)S(1)} %add.138), channel_id=1, source_target_pairs={{0,96},{1,97},{2,98},{3,99},{4,100},{5,101},{6,102},{7,103},{8,104... | collective-permute-start | bytes 442376 | tf_op jit(solution)/shard_map/ppermute | solution.py:282
  81.0 9.8 %collective-permute-start.17 = (f32[288,128]{1,0:T(8,128)S(1)}, f32[288,128]{1,0:T(8,128)S(1)}, u32[]{:S(2)}, u32[]{:S(2)}) collective-permute-start(f32[288,128]{1,0:T(8,128)S(1)} %add_add_fusion.2.sum_ref.refs_0_), channel_id=1, source_target_pairs={{0,16},{1,17},{2,18},{3,19},{4,20},{5,21},{6,22},{7,23},{8,24},{9,... | collective-permute-start | bytes 442376 | tf_op jit(solution)/shard_map/ppermute | solution.py:282
  94.4 17.9 %collective-permute-start.18 = (f32[288,128]{1,0:T(8,128)S(1)}, f32[288,128]{1,0:T(8,128)S(1)}, u32[]{:S(2)}, u32[]{:S(2)}) collective-permute-start(f32[288,128]{1,0:T(8,128)S(1)} %get-tuple-element.81), channel_id=1, source_target_pairs={{0,4},{1,5},{2,6},{3,7},{4,8},{5,9},{6,10},{7,11},{8,12},{9,13},{1... | collective-permute-start | bytes 442376 | tf_op jit(solution)/shard_map/ppermute | solution.py:282
  101.3 11.0 %collective-permute-start.19 = (f32[288,128]{1,0:T(8,128)S(1)}, f32[288,128]{1,0:T(8,128)S(1)}, u32[]{:S(2)}, u32[]{:S(2)}) collective-permute-start(f32[288,128]{1,0:T(8,128)S(1)} %get-tuple-element.82), channel_id=1, source_target_pairs={{0,8},{1,9},{2,10},{3,11},{4,12},{5,13},{6,14},{7,15},{8,0},{9,1},... | collective-permute-start | bytes 442376 | tf_op jit(solution)/shard_map/ppermute | solution.py:282
  106.2 6.1 %collective-permute-start.20 = (f32[288,128]{1,0:T(8,128)S(1)}, f32[288,128]{1,0:T(8,128)S(1)}, u32[]{:S(2)}, u32[]{:S(2)}) collective-permute-start(f32[288,128]{1,0:T(8,128)S(1)} %get-tuple-element.83), channel_id=1, source_target_pairs={{0,12},{1,13},{2,14},{3,15},{4,0},{5,1},{6,2},{7,3},{8,4},{9,5},{1... | collective-permute-start | bytes 442376 | tf_op jit(solution)/shard_map/ppermute | solution.py:282
  114.2 5.8 %collective-permute-start.22 = (f32[288,128]{1,0:T(8,128)S(1)}, f32[288,128]{1,0:T(8,128)S(1)}, u32[]{:S(2)}, u32[]{:S(2)}) collective-permute-start(f32[288,128]{1,0:T(8,128)S(1)} %add_add_fusion.1), channel_id=1, source_target_pairs={{0,2},{1,3},{2,0},{3,1},{4,6},{5,7},{6,4},{7,5},{8,10},{9,11},{10,... | collective-permute-start | bytes 442376 | tf_op jit(solution)/shard_map/ppermute | solution.py:282
  114.3 5.8 %collective-permute-start.23 = (f32[288,128]{1,0:T(8,128)S(1)}, f32[288,128]{1,0:T(8,128)S(1)}, u32[]{:S(2)}, u32[]{:S(2)}) collective-permute-start(f32[288,128]{1,0:T(8,128)S(1)} %add_add_fusion.1), channel_id=1, source_target_pairs={{0,3},{1,0},{2,1},{3,2},{4,7},{5,4},{6,5},{7,6},{8,11},{9,8},{10,9... | collective-permute-start | bytes 442376 | tf_op jit(solution)/shard_map/ppermute | solution.py:282
  120.1 15.4 %collective-permute-start.24 = (f32[288,128]{1,0:T(8,128)S(1)}, f32[288,128]{1,0:T(8,128)S(1)}, u32[]{:S(2)}, u32[]{:S(2)}) collective-permute-start(f32[288,128]{1,0:T(8,128)S(1)} %add_add_fusion.sum_ref.refs_0_), channel_id=1, source_target_pairs={{0,4},{1,5},{2,6},{3,7},{4,8},{5,9},{6,10},{7,11},{8,12},{9,13},{1... | collective-permute-start | bytes 442376 | tf_op jit(solution)/shard_map/ppermute | solution.py:282
  120.2 15.3 %collective-permute-start.25 = (f32[288,128]{1,0:T(8,128)S(1)}, f32[288,128]{1,0:T(8,128)}, u32[]{:S(2)}, u32[]{:S(2)}) collective-permute-start(f32[288,128]{1,0:T(8,128)S(1)} %add_add_fusion.sum_ref.refs_0_), channel_id=1, source_target_pairs={{0,8},{1,9},{2,10},{3,11},{4,12},{5,13},{6,14},{7,15},{8,0},{9,1},... | collective-permute-start | bytes 442376 | tf_op jit(solution)/shard_map/ppermute | solution.py:282
  122.2 13.3 %collective-permute-start.26 = (f32[288,128]{1,0:T(8,128)S(1)}, f32[288,128]{1,0:T(8,128)}, u32[]{:S(2)}, u32[]{:S(2)}) collective-permute-start(f32[288,128]{1,0:T(8,128)S(1)} %add_add_fusion.sum_ref.refs_0_), channel_id=1, source_target_pairs={{0,12},{1,13},{2,14},{3,15},{4,0},{5,1},{6,2},{7,3},{8,4},{9,5},{1... | collective-permute-start | bytes 442376 | tf_op jit(solution)/shard_map/ppermute | solution.py:282
  148.0 16.6 %collective-permute-start.28 = (f32[96,128]{1,0:T(8,128)S(1)}, f32[96,128]{1,0:T(8,128)S(1)}, u32[]{:S(2)}, u32[]{:S(2)}) collective-permute-start(f32[96,128]{1,0:T(8,128)S(1)} %get-tuple-element.98), channel_id=1, source_target_pairs={{0,32},{1,33},{2,34},{3,35},{4,36},{5,37},{6,38},{7,39},{8,40},{9,... | collective-permute-start | bytes 147464 | tf_op jit(solution)/shard_map/ppermute | solution.py:282
  148.4 16.3 %collective-permute-start.29 = (f32[96,128]{1,0:T(8,128)S(1)}, f32[96,128]{1,0:T(8,128)S(1)}, u32[]{:S(2)}, u32[]{:S(2)}) collective-permute-start(f32[96,128]{1,0:T(8,128)S(1)} %get-tuple-element.99), channel_id=1, source_target_pairs={{0,64},{1,65},{2,66},{3,67},{4,68},{5,69},{6,70},{7,71},{8,72},{9,... | collective-permute-start | bytes 147464 | tf_op jit(solution)/shard_map/ppermute | solution.py:282
  151.2 13.5 %collective-permute-start.30 = (f32[96,128]{1,0:T(8,128)S(1)}, f32[96,128]{1,0:T(8,128)S(1)}, u32[]{:S(2)}, u32[]{:S(2)}) collective-permute-start(f32[96,128]{1,0:T(8,128)S(1)} %get-tuple-element.100), channel_id=1, source_target_pairs={{0,96},{1,97},{2,98},{3,99},{4,100},{5,101},{6,102},{7,103},{8,104... | collective-permute-start | bytes 147464 | tf_op jit(solution)/shard_map/ppermute | solution.py:282
  (24 other events, 128.5 us)

commit v2 on v1

--- a/solution.py
+++ b/solution.py
@@ -2,6 +2,7 @@
 
 import jax
 import jax.numpy as jnp
+import numpy as np
 from jax import lax
 from jax.experimental import pallas as pl
 from jax.experimental.pallas import tpu as pltpu
@@ -53,6 +54,25 @@
     return jnp.concatenate([gram[:32], gram[32:]], axis=1)
 
 
+def solve_rows(rows, e):
+    n = len(rows)
+    for t in range(0, n, 2):
+        a, b, c, d = e[t][t], e[t][t + 1], e[t + 1][t], e[t + 1][t + 1]
+        scale = 1.0 / (a * d - b * c)
+        a, b, c, d = a * scale, b * scale, c * scale, d * scale
+        rows[t], rows[t + 1] = d * rows[t] - b * rows[t + 1], a * rows[t + 1] - c * rows[t]
+        for j in range(t + 2, n):
+            e[t][j], e[t + 1][j] = d * e[t][j] - b * e[t + 1][j], a * e[t + 1][j] - c * e[t][j]
+        for i in range(n):
+            if i in (t, t + 1):
+                continue
+            f, g = e[i][t], e[i][t + 1]
+            rows[i] = rows[i] - (f * rows[t] + g * rows[t + 1])
+            for j in range(t + 2, n):
+                e[i][j] = e[i][j] - (f * e[t][j] + g * e[t + 1][j])
+    return rows
+
+
 def inverse(packed):
     flat = jnp.concatenate([packed, pltpu.roll(packed, RANK, 1)], axis=0)
     row = lax.broadcasted_iota(jnp.int32, (RANK, 2 * RANK), 0)
@@ -60,42 +80,46 @@
     flat = jnp.where(lane < RANK, flat, 0.0)
     flat = flat + jnp.where(lane == row, RIDGE, 0.0)
     flat = flat + jnp.where(lane == row + RANK, 1.0, 0.0)
+    full = (8, 2 * RANK)
     blocks = [flat[8 * b : 8 * b + 8] for b in range(8)]
-    sub = lax.broadcasted_iota(jnp.int32, (8, 2 * RANK), 0)
-    for k in range(RANK):
-        b, s = divmod(k, 8)
-        pivot_row = jnp.broadcast_to(blocks[b][s : s + 1], (8, 2 * RANK))
-        pivot = jnp.broadcast_to(pivot_row[:, k : k + 1], (8, 2 * RANK))
-        scaled = pivot_row / pivot
+    sub = lax.broadcasted_iota(jnp.int32, full, 0)
+    for b in range(8):
+        k = 8 * b
+        rows = [jnp.broadcast_to(blocks[b][i : i + 1], full) for i in range(8)]
+        entries = [[jnp.broadcast_to(r[:, k + j : k + j + 1], full) for j in range(8)] for r in rows]
+        rows = solve_rows(rows, entries)
         for i in range(8):
-            column = jnp.broadcast_to(blocks[i][:, k : k + 1], (8, 2 * RANK))
-            changed = blocks[i] - column * scaled
-            if i == b:
-                changed = jnp.where(sub == s, scaled, changed)
+            changed = blocks[i]
+            for j in range(8):
+                if i == b:
+                    changed = jnp.where(sub == j, rows[j], changed)
+                else:
+                    changed = changed - jnp.broadcast_to(blocks[i][:, k + j : k + j + 1], full) * rows[j]
             blocks[i] = changed
     return jnp.concatenate(blocks, axis=0)
 
 
-def prep_kernel(chan_ref, time_ref, copies_ref, time_out):
-    rows = chan_ref[...]
-    packed = jnp.concatenate([rows[:RANK], rows[RANK:]], axis=1)
-    for i in range(16):
-        copies_ref[i] = packed
-    time_out[...] = time_ref[...].T
+def quarter_kernel(place_ref, *refs):
+    v = place_ref[3]
+    for k in range(4):
+        rows = pl.ds(pl.multiple_of(lax.rem(v + 4 - k, 4) * RANK, RANK), RANK)
+        piece = refs[k][...].T
+        refs[-1][rows] = jnp.concatenate([piece[:RANK], piece[RANK:]], axis=1)
 
 
 def right_kernel(start, place_ref, *refs):
     if start:
-        sources = refs[:4]
-        wide_ref, tall_ref, gram_ref, held = refs[4:]
+        owns, others = refs[:4], refs[4:8]
+        refs = refs[8:]
     else:
         mine_ref, other_ref, inv_ref = refs[:3]
-        wide_ref, tall_ref, gram_ref, held = refs[3:]
+        refs = refs[3:]
+    wide_ref, tall_ref, gram_ref, held = refs
     y, core = place_ref[0], place_ref[1]
     for k in range(4):
         spot = lax.rem(y + 4 - k, 4) if start else k
         if start:
-            own, other = sources[k][:RANK], sources[k][RANK:]
+            own, other = owns[k][...], others[k][...]
         else:
             own, other = mine_ref[RANK * k : RANK * (k + 1)], other_ref[RANK * k : RANK * (k + 1)]
         held[2 * spot + core] = own
@@ -117,7 +141,7 @@
     return jnp.where(core == 0, 4 * q + i, 4 * i + q)
 
 
-def rows_kernel(start, j, place_ref, a_ref, left_ref, wide_ref, tall_ref, gram_ref, s_ref, h_ref, l_ref):
+def rows_kernel(j, place_ref, a_ref, left_ref, wide_ref, tall_ref, gram_ref, s_ref, h_ref, l_ref):
     core, u = place_ref[1], place_ref[2]
     q = lax.rem(u + j + 1, 4)
     low = low_lanes((RANK, PIECE))
@@ -127,24 +151,20 @@
         for i in (2 * half, 2 * half + 1):
             p = piece_of(core, q, i)
             spots.append(pl.multiple_of(p * PIECE, PIECE))
-            packed = left_ref[p] if start else left_ref[RANK * i : RANK * (i + 1)]
+            packed = left_ref[RANK * i : RANK * (i + 1)]
             stacks.append(row_stack(packed))
         stack = jnp.concatenate(stacks, axis=0)
         stack = jnp.concatenate([stack, stack], axis=1)
-        total = jnp.zeros((256, PIECE), F32)
-        for t in range(4):
-            cols = slice(256 * t, 256 * t + 256)
-            product = single(stack, wide_ref[:, cols], ((1,), (0,)))
-            values = jnp.concatenate([a_ref[pl.ds(s, PIECE), cols] for s in spots], axis=0)
-            cleaned = product + jnp.clip(values - product, -THRESHOLD, THRESHOLD)
-            high, rest = two_parts(cleaned)
-            for n in range(2):
-                i = 2 * half + n
-                for part, ref in ((high, h_ref), (rest, l_ref)):
-                    ref[64 * i : 64 * i + 64, cols] = part[128 * n : 128 * n + 64]
-                    ref[256 + 64 * i : 320 + 64 * i, cols] = part[128 * n + 64 : 128 * n + 128]
-            total += single(high, tall_ref[:, cols], ((1,), (1,)))
-            total += single(rest, tall_ref[:, cols], ((1,), (1,)))
+        product = single(stack, wide_ref[...], ((1,), (0,)))
+        values = jnp.concatenate([a_ref[pl.ds(s, PIECE)] for s in spots], axis=0)
+        cleaned = product + jnp.clip(values - product, -THRESHOLD, THRESHOLD)
+        high, rest = two_parts(cleaned)
+        for n in range(2):
+            i = 2 * half + n
+            for part, ref in ((high, h_ref), (rest, l_ref)):
+                ref[64 * i : 64 * i + 64] = part[128 * n : 128 * n + 64]
+                ref[256 + 64 * i : 320 + 64 * i] = part[128 * n + 64 : 128 * n + 128]
+        total = single(high, tall_ref[...], ((1,), (1,))) + single(rest, tall_ref[...], ((1,), (1,)))
         total = total + pltpu.roll(total, RANK, 1)
         for n in range(2):
             i = 2 * half + n
@@ -153,7 +173,7 @@
 
 
 def inverse_kernel(sum_ref, inv_ref):
-    found = inverse(sum_ref[256:288])
+    found = inverse(sum_ref[...])
     low = low_lanes((RANK, PIECE))
     inv_ref[0:64] = jnp.where(low, pltpu.roll(found, RANK, 1), 0.0)
     inv_ref[64:128] = jnp.where(low, 0.0, found)
@@ -181,7 +201,7 @@
             held = left_refs[1]
             held[...] = packed
             own = held[pl.ds(pl.multiple_of(v * RANK, RANK), RANK)]
-            left_refs[0][...] = jnp.concatenate([own[:, :RANK], own[:, RANK:]], axis=0)
+            left_refs[0][...] = jnp.concatenate([own[:, :RANK], own[:, RANK:]], axis=0).T
         turned = packed.T
         turned = jnp.concatenate([turned[:RANK], turned[RANK:]], axis=1)
         gram += exact(turned, turned, ((1,), (1,)))
@@ -221,21 +241,36 @@
 def final_kernel(m0, m1, m2, m3, out_ref):
     total = m0[...] + m1[...] + m2[...] + m3[...]
     found = inverse(total[64:96])[:, RANK:]
-    out_ref[...] = exact(found, total[:64], ((1,), (0,))).T
-
-
-def outlier_kernel(spots_ref, left_ref, wide_ref, a_ref, out_ref):
+    out_ref[...] = exact(found, total[:64], ((1,), (0,)))
+
+
+def outlier_kernel(spots_ref, left_ref, wide_ref, a_ref, after_ref, out_ref, token_ref):
     g = pl.program_id(0)
-    stack = row_stack(left_ref[pl.ds(pl.multiple_of(g * RANK, RANK), RANK)])
+    stacks = []
+    for n in range(2):
+        spot = pl.multiple_of(spots_ref[4 + 2 * g + n] * RANK, RANK)
+        stacks.append(row_stack(left_ref[pl.ds(spot, RANK)]))
+    stack = jnp.concatenate(stacks, axis=0)
     stack = jnp.concatenate([stack, stack], axis=1)
-    for t in range(4):
-        cols = slice(256 * t, 256 * t + 256)
-        residue = a_ref[:, cols] - single(stack, wide_ref[:, cols], ((1,), (0,)))
+    rows = pl.ds(pl.multiple_of(g * 256, 256), 256)
+    for t in range(2):
+        cols = slice(512 * t, 512 * t + 512)
+        residue = a_ref[rows, cols] - single(stack, wide_ref[:, cols], ((1,), (0,)))
         out_ref[:, cols] = residue - jnp.clip(residue, -THRESHOLD, THRESHOLD)
+    token_ref[...] = jnp.zeros_like(token_ref)
+
+
+def sum_kernel(count, *refs):
+    total = refs[0][...]
+    for ref in refs[1:count]:
+        total = total + ref[...]
+    refs[-2][...] = total[:256]
+    refs[-1][...] = total[256:]
 
 
 VM = pl.BlockSpec(memory_space=pltpu.VMEM)
 SM = pl.BlockSpec(memory_space=pltpu.SMEM)
+ANY = pl.BlockSpec(memory_space=pl.ANY)
 
 
 def shape(*dims, dtype=F32):
@@ -282,24 +317,34 @@
     return lax.ppermute(values, AXES, ring(kind, k))
 
 
-def sum_around(values, kind):
-    return values + send(values, kind, 1) + send(values, kind, 2) + send(values, kind, 3)
+def places():
+    table = np.zeros((128, 20), np.int32)
+    for chan in range(8):
+        for tm in range(16):
+            y, core = divmod(chan, 2)
+            x, z = divmod(tm, 4)
+            u, v = (x, z) if core == 0 else (z, x)
+            spots = []
+            for p in range(16):
+                q, i = divmod(p, 4)
+                if core == 1:
+                    q, i = i, q
+                spots.append((u - q) % 4 * 4 + i)
+            table[chan * 16 + tm] = [y, core, u, v] + spots
+    return table
 
 
 def shards(readings, channel_start, time_start):
     chan, tm = lax.axis_index("chan"), lax.axis_index("tm")
-    y, core, x, z = chan // 2, chan % 2, tm // 4, tm % 4
-    u, v = jnp.where(core == 0, x, z), jnp.where(core == 0, z, x)
-    place = jnp.stack([y, core, u, v]).astype(jnp.int32)
-    values = readings
-
-    copies, time_piece = call(prep_kernel, [shape(16, 64, 128), shape(64, 128)], [channel_start, time_start], name="prep")
-    pair = jnp.concatenate([time_piece, send(time_piece, "core")], axis=0)
-    around = [pair] + [send(pair, "y", k) for k in (1, 2, 3)]
-    lefts = lax.all_to_all(copies, "tm", split_axis=0, concat_axis=0, tiled=True)
-    lefts = [lefts] * 4
-
-    right_args = around
+    place = lax.dynamic_index_in_dim(jnp.asarray(places()), chan * 16 + tm, keepdims=False)
+
+    chan_piece, time_piece = channel_start.T, time_start.T
+    lefts = [chan_piece] + [send(chan_piece, "v", k) for k in (1, 2, 3)]
+    owns = [time_piece] + [send(time_piece, "y", k) for k in (1, 2, 3)]
+    (left_own,) = call(quarter_kernel, [shape(256, 128)], [place] + lefts + owns[1:], name="quarter", flops=5 * 10**9)
+    lefts = [left_own] + [send(left_own, "u", k) for k in (1, 2, 3)]
+    others = [send(piece, "core") for piece in owns]
+    right_args = owns + others
     for sweep in range(2):
         start, last = sweep == 0, sweep == 1
         wide, tall, gram = call(
@@ -308,13 +353,14 @@
             [place] + list(right_args),
             scratch=[pltpu.VMEM((8, 64, 128), F32)],
             name="right",
+            flops=5 * 10**9,
         )
         sums, highs, rests = [], [], []
         for j in range(4):
             s, h, r = call(
-                functools.partial(rows_kernel, start, j),
-                [shape(288, 128), shape(512, 1024, dtype=BF16), shape(512, 1024, dtype=BF16)],
-                [place, values, lefts[3 - j], wide, tall, gram],
+                functools.partial(rows_kernel, j),
+                [shape(288, 128), pltpu.VMEM((512, 1024), BF16), pltpu.VMEM((512, 1024), BF16)],
+                [place, readings, lefts[3 - j], wide, tall, gram],
                 name="rows",
                 flops=2 * 512 * 1024 * 768,
             )
@@ -323,15 +369,36 @@
             rests.append(r)
         got = [send(sums[k - 1], "u", k) for k in (1, 2, 3)]
         own = sums[3] + got[0] + got[1] + got[2]
-        own = sum_around(own, "v")
-        (inv,) = call(inverse_kernel, [shape(128, 128)], [own], name="inverse", flops=10**9)
+        if last:
+            outliers, token = pl.pallas_call(
+                outlier_kernel,
+                out_shape=[shape(2048, 1024), shape(8, 128)],
+                grid_spec=pltpu.PrefetchScalarGridSpec(
+                    num_scalar_prefetch=1,
+                    grid=(8,),
+                    in_specs=[
+                        pl.BlockSpec((1024, 128), lambda g, spots: (0, 0)),
+                        pl.BlockSpec((256, 1024), lambda g, spots: (0, 0)),
+                        VM,
+                        ANY,
+                    ],
+                    out_specs=[
+                        pl.BlockSpec((256, 1024), lambda g, spots: (g, 0)),
+                        pl.BlockSpec((8, 128), lambda g, spots: (0, 0)),
+                    ],
+                ),
+                compiler_params=pltpu.CompilerParams(vmem_limit_bytes=12 * MIB),
+                cost_estimate=pl.CostEstimate(flops=2 * 2048 * 1024 * 256, bytes_accessed=16 * MIB, transcendentals=0),
+                name="outliers",
+            )(place, jnp.concatenate(lefts, axis=0), wide, readings, own)
+        parts = [own] + [send(own, "v", k) for k in (1, 2, 3)]
+        own, gram = call(functools.partial(sum_kernel, 4), [shape(256, 128), shape(32, 128)], parts + ([token] if last else []), name="sum")
+        (inv,) = call(inverse_kernel, [shape(128, 128)], [gram], name="inverse", flops=10**9)
         quarters = [own] + [send(own, "u", k) for k in (1, 2, 3)]
-        if last:
-            left_all = jnp.concatenate(lefts, axis=0)
         first_outs = [shape(64, 1024), shape(64, 64)]
         first_scratch = []
         if last:
-            first_outs.append(shape(128, 64))
+            first_outs.append(shape(64, 128))
             first_scratch.append(pltpu.VMEM((256, 128), F32))
         else:
             first_outs.append(shape(256, 128))
@@ -354,35 +421,17 @@
         )
         swapped = send(other, "core")
         if not last:
-            half = sum_around(mine + swapped, "y")
-            (inv,) = call(inverse_kernel, [shape(128, 128)], [half], name="inverse", flops=10**9)
+            half = mine + swapped
+            parts = [half] + [send(half, "y", k) for k in (1, 2, 3)]
+            half, gram = call(functools.partial(sum_kernel, 4), [shape(256, 128), shape(32, 128)], parts, name="sum")
+            (inv,) = call(inverse_kernel, [shape(128, 128)], [gram], name="inverse", flops=10**9)
             right_args = [half, send(half, "core"), inv]
             lefts = [first_left] + list(more)
     messages = call(message_kernel, [shape(96, 128)] * 4, [place, mine, swapped], name="messages")
     parts = [messages[0]] + [send(messages[k], "y", k) for k in (1, 2, 3)]
-    (time_out,) = call(final_kernel, [shape(128, 64)], parts, name="final")
-
-    q = jnp.stack([(u + 4 - g // 4) % 4 for g in range(16)])
-    i = jnp.arange(16) % 4
-    spots = jnp.where(core == 0, 4 * q + i, 4 * i + q).astype(jnp.int32)
-    outliers = pl.pallas_call(
-        outlier_kernel,
-        out_shape=shape(2048, 1024),
-        grid_spec=pltpu.PrefetchScalarGridSpec(
-            num_scalar_prefetch=1,
-            grid=(16,),
-            in_specs=[
-                pl.BlockSpec((1024, 128), lambda g, spots: (0, 0)),
-                pl.BlockSpec((256, 1024), lambda g, spots: (0, 0)),
-                pl.BlockSpec((128, 1024), lambda g, spots: (spots[g], 0)),
-            ],
-            out_specs=pl.BlockSpec((128, 1024), lambda g, spots: (spots[g], 0)),
-        ),
-        compiler_params=pltpu.CompilerParams(vmem_limit_bytes=16 * MIB),
-        cost_estimate=pl.CostEstimate(flops=2 * 2048 * 1024 * 256, bytes_accessed=16 * MIB, transcendentals=0),
-        name="outliers",
-    )(spots, left_all, wide, readings)
-    return outliers, first_left, time_out
+    (time_out,) = call(final_kernel, [shape(64, 128)], parts, name="final")
+
+    return outliers, first_left.T, time_out.T
 
 
 def solution(mesh):

time: 175 us -> 131 us (0.75)
  Pallas kernels: 72.9 us -> 42.9 us
  local copies, waits for them, and re-layouts: 23.2 us -> 1.46 us
  waiting for transfers between devices: 18.8 us -> 23.8 us
  starting transfers between devices: 58 us -> 61.4 us
    pallas_call x20 -> x23, Pallas kernels: 63.5 us -> 36.7 us  [call(): pl.pallas_call(kernel, out_shape=outs, in_specs=[SM if a.dtype == jnp.int...]
    unnamed x37 -> x8, local copies, waits for them, and re-layouts: 23.1 us -> 0.77 us
    ppermute x31 -> x40, starting transfers between devices: 49.5 us -> 61.4 us  [send(): return lax.ppermute(values, AXES, ring(kind, k))]
    all_to_all x1 -> x0, starting transfers between devices: 8.43 us -> none  [shards(): lax.all_to_all(copies, 'tm', split_axis=0, concat_axis=0, tiled=True)]
    ppermute x31 -> x40, waiting for transfers between devices: 18.7 us -> 23.8 us  [send(): return lax.ppermute(values, AXES, ring(kind, k))]
    pallas_call x1, Pallas kernels: 9.42 us -> 6.21 us  [shards(): pl.pallas_call(outlier_kernel, out_shape=[shape(2048, 1024), shape(8, 128...]
  transfers between devices with their start and end apart: 32 -> 40, of which waited for: 15 -> 16; matrix products, arithmetic and copies ran while one was open for 1% -> 1% of each run, Pallas kernels for 30% -> 24%
where the time goes in v2:
time: 131 us
  starting transfers between devices  61.4 us (47%)
  Pallas kernels  42.9 us (33%)
  waiting for transfers between devices  23.8 us (18%)
  local copies, waits for them, and re-layouts  1.46 us (1%)
    ppermute x40, starting transfers between devices, send(): return lax.ppermute(values, AXES, ring(kind, k))  61.4 us
    pallas_call x23, Pallas kernels, call(): pl.pallas_call(kernel, out_shape=outs, in_specs=[SM if a.dtype == jnp.int...  36.7 us
    ppermute x40, waiting for transfers between devices, send(): return lax.ppermute(values, AXES, ring(kind, k))  23.8 us
    pallas_call x1, Pallas kernels, shards(): pl.pallas_call(outlier_kernel, out_shape=[shape(2048, 1024), shape(8, 128...  6.21 us
  transfers between devices with their start and end apart: 40, of which 16 were waited for; matrix products, arithmetic and copies ran while one was open for 1% of the time, Pallas kernels for 24%

profile of v2, /device:TPU:1, one launch (start us, length us, event | category | flops | bytes accessed | tf_op | source)
XLA Modules:
  0.0 130.5 jit_solution(606010388578518644)
XLA Ops:
  0.6 2.2 %collective-permute-start.3 = (f32[64,128]{1,0:T(8,128)}, f32[64,128]{1,0:T(8,128)S(1)}, u32[]{:S(2)}, u32[]{:S(2)}) collective-permute-start(f32[64,128]{1,0:T(8,128)} %bitcast.12), channel_id=1, source_target_pairs={{0,32},{1,33},{2,34},{3,35},{4,36},{5,37},{6,38},{7,39},{8,40},{9,... | collective-permute-start | bytes 98312 | tf_op jit(solution)/shard_map/ppermute | solution.py:317
  2.8 2.6 %collective-permute-start.4 = (f32[64,128]{1,0:T(8,128)}, f32[64,128]{1,0:T(8,128)S(1)}, u32[]{:S(2)}, u32[]{:S(2)}) collective-permute-start(f32[64,128]{1,0:T(8,128)} %bitcast.13), channel_id=1, source_target_pairs={{0,64},{1,65},{2,66},{3,67},{4,68},{5,69},{6,70},{7,71},{8,72},{9,... | collective-permute-start | bytes 98312 | tf_op jit(solution)/shard_map/ppermute | solution.py:317
  7.7 2.5 %collective-permute-start.1 = (f32[64,128]{1,0:T(8,128)}, f32[64,128]{1,0:T(8,128)S(1)}, u32[]{:S(2)}, u32[]{:S(2)}) collective-permute-start(f32[64,128]{1,0:T(8,128)} %bitcast.9), channel_id=1, source_target_pairs={{0,2},{1,3},{2,0},{3,1},{4,6},{5,7},{6,4},{7,5},{8,10},{9,11},{10,... | collective-permute-start | bytes 98312 | tf_op jit(solution)/shard_map/ppermute | solution.py:317
  12.0 3.2 %collective-permute-start.6 = (f32[64,128]{1,0:T(8,128)}, f32[64,128]{1,0:T(8,128)S(1)}, u32[]{:S(2)}, u32[]{:S(2)}) collective-permute-start(f32[64,128]{1,0:T(8,128)} %bitcast.15), channel_id=1, source_target_pairs={{0,16},{1,17},{2,18},{3,19},{4,20},{5,21},{6,22},{7,23},{8,24},{9,... | collective-permute-start | bytes 98312 | tf_op jit(solution)/shard_map/ppermute | solution.py:317
  26.9 2.7 %collective-permute-start.13 = (f32[288,128]{1,0:T(8,128)S(1)}, f32[288,128]{1,0:T(8,128)S(1)}, u32[]{:S(2)}, u32[]{:S(2)}) collective-permute-start(f32[288,128]{1,0:T(8,128)S(1)} %get-tuple-element.63), channel_id=1, source_target_pairs={{0,8},{1,9},{2,10},{3,11},{4,12},{5,13},{6,14},{7,15},{8,0},{9,1},... | collective-permute-start | bytes 442376 | tf_op jit(solution)/shard_map/ppermute | solution.py:317
  37.2 2.4 %collective-permute-start.17 = (f32[288,128]{1,0:T(8,128)S(1)}, f32[288,128]{1,0:T(8,128)S(1)}, u32[]{:S(2)}, u32[]{:S(2)}) collective-permute-start(f32[288,128]{1,0:T(8,128)S(1)} %add_add_fusion.1.refs_0_), channel_id=1, source_target_pairs={{0,2},{1,3},{2,0},{3,1},{4,6},{5,7},{6,4},{7,5},{8,10},{9,11},{10,... | collective-permute-start | bytes 442376 | tf_op jit(solution)/shard_map/ppermute | solution.py:317
  41.0 2.8 %collective-permute-done.17.refs_2_ = f32[288,128]{1,0:T(8,128)S(1)} collective-permute-done((f32[288,128]{1,0:T(8,128)S(1)}, f32[288,128]{1,0:T(8,128)S(1)}, u32[]{:S(2)}, u32[]{:S(2)}) %collective-permute-start.17) | collective-permute-done | bytes 147488 | tf_op jit(solution)/shard_map/ppermute | solution.py:317
  44.8 3.1 %collective-permute-start.20 = (f32[256,128]{1,0:T(8,128)S(1)}, f32[256,128]{1,0:T(8,128)S(1)}, u32[]{:S(2)}, u32[]{:S(2)}) collective-permute-start(f32[256,128]{1,0:T(8,128)S(1)} %get-tuple-element.66.refs_0_), channel_id=1, source_target_pairs={{0,8},{1,9},{2,10},{3,11},{4,12},{5,13},{6,14},{7,15},{8,0},{9,1},... | collective-permute-start | bytes 393224 | tf_op jit(solution)/shard_map/ppermute | solution.py:317
  47.9 2.0 %inverse.3.inv_ref = f32[128,128]{1,0:T(8,128)S(1)} custom-call(f32[32,128]{1,0:T(8,128)S(1)} %get-tuple-element.65.sum_ref), custom_call_target="tpu_custom_call" | custom-call | flops 1000000000 | bytes 1048576 | tf_op jit(solution)/shard_map/inverse/pallas_call | solution.py:281
  55.0 2.5 %cols_rest.2 = (f32[288,128]{1,0:T(8,128)S(1)}, f32[288,128]{1,0:T(8,128)S(1)}, f32[256,128]{1,0:T(8,128)S(1)}, f32[256,128]{1,0:T(8,128)S(1)}, f32[256,128]{1,0:T(8,128)S(1)}) custom-call(s32[20]{0:T(128)S(1)} %dynamic-slice_bitcast_fusion.place_ref.spots_ref, f32[128,128]{1,0:T(8,128)S(1)} %inverse.3.inv_ref, ...), custom_call_target="tpu_custom_call" | custom-call | flops 805306368 | bytes 1048576 | tf_op jit(solution)/shard_map/cols_rest/pallas_call | solution.py:281
  57.5 9.2 %collective-permute-start.22 = (f32[288,128]{1,0:T(8,128)S(1)}, f32[288,128]{1,0:T(8,128)S(1)}, u32[]{:S(2)}, u32[]{:S(2)}) collective-permute-start(f32[288,128]{1,0:T(8,128)S(1)} %get-tuple-element.82), channel_id=1, source_target_pairs={{0,16},{1,17},{2,18},{3,19},{4,20},{5,21},{6,22},{7,23},{8,24},{9,... | collective-permute-start | bytes 442376 | tf_op jit(solution)/shard_map/ppermute | solution.py:317
  70.6 6.6 %collective-permute-done.23.refs_1_ = f32[288,128]{1,0:T(8,128)S(1)} collective-permute-done((f32[288,128]{1,0:T(8,128)S(1)}, f32[288,128]{1,0:T(8,128)S(1)}, u32[]{:S(2)}, u32[]{:S(2)}) %collective-permute-start.23) | collective-permute-done | bytes 147488 | tf_op jit(solution)/shard_map/ppermute | solution.py:317
  79.1 2.0 %inverse.4.refs_2_ = f32[128,128]{1,0:T(8,128)S(1)} custom-call(f32[32,128]{1,0:T(8,128)S(1)} %get-tuple-element.84.sum_ref), custom_call_target="tpu_custom_call" | custom-call | flops 1000000000 | bytes 1048576 | tf_op jit(solution)/shard_map/inverse/pallas_call | solution.py:281
  86.8 3.5 %collective-permute-start.28 = (f32[288,128]{1,0:T(8,128)S(1)}, f32[288,128]{1,0:T(8,128)S(1)}, u32[]{:S(2)}, u32[]{:S(2)}) collective-permute-start(f32[288,128]{1,0:T(8,128)S(1)} %get-tuple-element.90), channel_id=1, source_target_pairs={{0,8},{1,9},{2,10},{3,11},{4,12},{5,13},{6,14},{7,15},{8,0},{9,1},... | collective-permute-start | bytes 442376 | tf_op jit(solution)/shard_map/ppermute | solution.py:317
  94.3 2.3 %collective-permute-done.29 = f32[288,128]{1,0:T(8,128)S(1)} collective-permute-done((f32[288,128]{1,0:T(8,128)S(1)}, f32[288,128]{1,0:T(8,128)S(1)}, u32[]{:S(2)}, u32[]{:S(2)}) %collective-permute-start.29) | collective-permute-done | bytes 147488 | tf_op jit(solution)/shard_map/ppermute | solution.py:317
  97.0 2.7 %collective-permute-start.31 = (f32[288,128]{1,0:T(8,128)S(1)}, f32[288,128]{1,0:T(8,128)S(1)}, u32[]{:S(2)}, u32[]{:S(2)}) collective-permute-start(f32[288,128]{1,0:T(8,128)S(1)} %add_add_fusion.after_ref.refs_0_), channel_id=1, source_target_pairs={{0,2},{1,3},{2,0},{3,1},{4,6},{5,7},{6,4},{7,5},{8,10},{9,11},{10,... | collective-permute-start | bytes 442376 | tf_op jit(solution)/shard_map/ppermute | solution.py:317
  99.7 6.2 %outliers.1 = (f32[2048,1024]{1,0:T(8,128)}, f32[8,128]{1,0:T(8,128)S(1)}) custom-call(s32[20]{0:T(128)S(1)} %dynamic-slice_bitcast_fusion.place_ref.spots_ref, f32[1024,128]{1,0:T(8,128)S(1)} %pad_maximum_fusion.left_ref, bf16[256,1024]{1,0:T(8,128)(2,1)S(1)} %get-tuple-element.85.wide_ref, f32[2048,1024]{1,0:T(8,128)S(1)} %bitcast.7, ...), custom_call_target="tpu_custom_call" | custom-call | flops 1073741824 | bytes 16777216 | tf_op jit(solution)/shard_map/outliers/pallas_call | solution.py:373
  106.1 2.7 %collective-permute-start.34 = (f32[256,128]{1,0:T(8,128)S(1)}, f32[256,128]{1,0:T(8,128)S(1)}, u32[]{:S(2)}, u32[]{:S(2)}) collective-permute-start(f32[256,128]{1,0:T(8,128)S(1)} %get-tuple-element.95.refs_0_), channel_id=1, source_target_pairs={{0,8},{1,9},{2,10},{3,11},{4,12},{5,13},{6,14},{7,15},{8,0},{9,1},... | collective-permute-start | bytes 393224 | tf_op jit(solution)/shard_map/ppermute | solution.py:317
  108.7 2.0 %inverse.5.inv_ref = f32[128,128]{1,0:T(8,128)S(1)} custom-call(f32[32,128]{1,0:T(8,128)S(1)} %get-tuple-element.94.sum_ref), custom_call_target="tpu_custom_call" | custom-call | flops 1000000000 | bytes 1048576 | tf_op jit(solution)/shard_map/inverse/pallas_call | solution.py:281
  110.7 2.1 %cols_own.3 = (f32[64,1024]{1,0:T(8,128)S(1)}, f32[64,64]{1,0:T(8,128)S(1)}, f32[64,128]{1,0:T(8,128)}) custom-call(s32[20]{0:T(128)S(1)} %dynamic-slice_bitcast_fusion.place_ref.spots_ref, f32[128,128]{1,0:T(8,128)S(1)} %inverse.5.inv_ref, f32[256,128]{1,0:T(8,128)S(1)} %get-tuple-element.95.refs_0_, bf16[512,1024]{1,0:T(8,128)(2,1)S(1)} %get-tuple-element.96.refs_1_, ...), custom_call_target="tpu_custom_call" | custom-call | flops 268435456 | bytes 1048576 | tf_op jit(solution)/shard_map/cols_own/pallas_call | solution.py:281
  113.4 2.5 %cols_rest.3 = (f32[288,128]{1,0:T(8,128)S(1)}, f32[288,128]{1,0:T(8,128)S(1)}) custom-call(s32[20]{0:T(128)S(1)} %dynamic-slice_bitcast_fusion.place_ref.spots_ref, f32[128,128]{1,0:T(8,128)S(1)} %inverse.5.inv_ref, f32[256,128]{1,0:T(8,128)S(1)} %collective-permute-done.33.refs_0_, f32[256,128]{1,0:T(8,128)S(1)} %collective-permute-done.34.refs_1_, ...), custom_call_target="tpu_custom_call" | custom-call | flops 805306368 | bytes 1048576 | tf_op jit(solution)/shard_map/cols_rest/pallas_call | solution.py:281
  115.9 3.5 %collective-permute-start.36 = (f32[288,128]{1,0:T(8,128)S(1)}, f32[288,128]{1,0:T(8,128)S(1)}, u32[]{:S(2)}, u32[]{:S(2)}) collective-permute-start(f32[288,128]{1,0:T(8,128)S(1)} %get-tuple-element.108), channel_id=1, source_target_pairs={{0,16},{1,17},{2,18},{3,19},{4,20},{5,21},{6,22},{7,23},{8,24},{9,... | collective-permute-start | bytes 442376 | tf_op jit(solution)/shard_map/ppermute | solution.py:317
  121.2 3.3 %collective-permute-start.38 = (f32[96,128]{1,0:T(8,128)S(1)}, f32[96,128]{1,0:T(8,128)S(1)}, u32[]{:S(2)}, u32[]{:S(2)}) collective-permute-start(f32[96,128]{1,0:T(8,128)S(1)} %get-tuple-element.111), channel_id=1, source_target_pairs={{0,64},{1,65},{2,66},{3,67},{4,68},{5,69},{6,70},{7,71},{8,72},{9,... | collective-permute-start | bytes 147464 | tf_op jit(solution)/shard_map/ppermute | solution.py:317
  127.7 2.8 %final.1 = f32[64,128]{1,0:T(8,128)} custom-call(f32[96,128]{1,0:T(8,128)S(1)} %get-tuple-element.109.m0, f32[96,128]{1,0:T(8,128)S(1)} %collective-permute-done.37.m1, f32[96,128]{1,0:T(8,128)S(1)} %collective-permute-done.38.m2, f32[96,128]{1,0:T(8,128)S(1)} %collective-permute-done.39.m3), custom_call_target="tpu_custom_call" | custom-call | bytes 1048576 | tf_op jit(solution)/shard_map/final/pallas_call | solution.py:281
  (94 shorter events, 52.3 us)
Async XLA Ops:
  0.6 9.6 %collective-permute-start.3 = (f32[64,128]{1,0:T(8,128)}, f32[64,128]{1,0:T(8,128)S(1)}, u32[]{:S(2)}, u32[]{:S(2)}) collective-permute-start(f32[64,128]{1,0:T(8,128)} %bitcast.12), channel_id=1, source_target_pairs={{0,32},{1,33},{2,34},{3,35},{4,36},{5,37},{6,38},{7,39},{8,40},{9,... | collective-permute-start | bytes 98312 | tf_op jit(solution)/shard_map/ppermute | solution.py:317
  2.8 9.2 %collective-permute-start.4 = (f32[64,128]{1,0:T(8,128)}, f32[64,128]{1,0:T(8,128)S(1)}, u32[]{:S(2)}, u32[]{:S(2)}) collective-permute-start(f32[64,128]{1,0:T(8,128)} %bitcast.13), channel_id=1, source_target_pairs={{0,64},{1,65},{2,66},{3,67},{4,68},{5,69},{6,70},{7,71},{8,72},{9,... | collective-permute-start | bytes 98312 | tf_op jit(solution)/shard_map/ppermute | solution.py:317
  5.4 9.8 %collective-permute-start.5 = (f32[64,128]{1,0:T(8,128)}, f32[64,128]{1,0:T(8,128)S(1)}, u32[]{:S(2)}, u32[]{:S(2)}) collective-permute-start(f32[64,128]{1,0:T(8,128)} %bitcast.14), channel_id=1, source_target_pairs={{0,96},{1,97},{2,98},{3,99},{4,100},{5,101},{6,102},{7,103},{8,104... | collective-permute-start | bytes 98312 | tf_op jit(solution)/shard_map/ppermute | solution.py:317
  6.5 8.8 %collective-permute-start = (f32[64,128]{1,0:T(8,128)}, f32[64,128]{1,0:T(8,128)S(1)}, u32[]{:S(2)}, u32[]{:S(2)}) collective-permute-start(f32[64,128]{1,0:T(8,128)} %bitcast.8), channel_id=1, source_target_pairs={{0,1},{1,2},{2,3},{3,0},{4,5},{5,6},{6,7},{7,4},{8,9},{9,10},{10,1... | collective-permute-start | bytes 98312 | tf_op jit(solution)/shard_map/ppermute | solution.py:317
  7.7 8.0 %collective-permute-start.1 = (f32[64,128]{1,0:T(8,128)}, f32[64,128]{1,0:T(8,128)S(1)}, u32[]{:S(2)}, u32[]{:S(2)}) collective-permute-start(f32[64,128]{1,0:T(8,128)} %bitcast.9), channel_id=1, source_target_pairs={{0,2},{1,3},{2,0},{3,1},{4,6},{5,7},{6,4},{7,5},{8,10},{9,11},{10,... | collective-permute-start | bytes 98312 | tf_op jit(solution)/shard_map/ppermute | solution.py:317
  12.0 7.0 %collective-permute-start.6 = (f32[64,128]{1,0:T(8,128)}, f32[64,128]{1,0:T(8,128)S(1)}, u32[]{:S(2)}, u32[]{:S(2)}) collective-permute-start(f32[64,128]{1,0:T(8,128)} %bitcast.15), channel_id=1, source_target_pairs={{0,16},{1,17},{2,18},{3,19},{4,20},{5,21},{6,22},{7,23},{8,24},{9,... | collective-permute-start | bytes 98312 | tf_op jit(solution)/shard_map/ppermute | solution.py:317
  20.6 8.9 %collective-permute-start.14 = (f32[256,128]{1,0:T(8,128)S(1)}, f32[256,128]{1,0:T(8,128)S(1)}, u32[]{:S(2)}, u32[]{:S(2)}) collective-permute-start(f32[256,128]{1,0:T(8,128)S(1)} %quarter.1.left_ref), channel_id=1, source_target_pairs={{0,4},{1,5},{2,6},{3,7},{4,8},{5,9},{6,10},{7,11},{8,12},{9,13},{1... | collective-permute-start | bytes 393224 | tf_op jit(solution)/shard_map/ppermute | solution.py:317
  24.4 10.2 %collective-permute-start.11 = (f32[288,128]{1,0:T(8,128)S(1)}, f32[288,128]{1,0:T(8,128)S(1)}, u32[]{:S(2)}, u32[]{:S(2)}) collective-permute-start(f32[288,128]{1,0:T(8,128)S(1)} %get-tuple-element.62), channel_id=1, source_target_pairs={{0,4},{1,5},{2,6},{3,7},{4,8},{5,9},{6,10},{7,11},{8,12},{9,13},{1... | collective-permute-start | bytes 442376 | tf_op jit(solution)/shard_map/ppermute | solution.py:317
  26.9 7.7 %collective-permute-start.13 = (f32[288,128]{1,0:T(8,128)S(1)}, f32[288,128]{1,0:T(8,128)S(1)}, u32[]{:S(2)}, u32[]{:S(2)}) collective-permute-start(f32[288,128]{1,0:T(8,128)S(1)} %get-tuple-element.63), channel_id=1, source_target_pairs={{0,8},{1,9},{2,10},{3,11},{4,12},{5,13},{6,14},{7,15},{8,0},{9,1},... | collective-permute-start | bytes 442376 | tf_op jit(solution)/shard_map/ppermute | solution.py:317
  37.2 6.6 %collective-permute-start.17 = (f32[288,128]{1,0:T(8,128)S(1)}, f32[288,128]{1,0:T(8,128)S(1)}, u32[]{:S(2)}, u32[]{:S(2)}) collective-permute-start(f32[288,128]{1,0:T(8,128)S(1)} %add_add_fusion.1.refs_0_), channel_id=1, source_target_pairs={{0,2},{1,3},{2,0},{3,1},{4,6},{5,7},{6,4},{7,5},{8,10},{9,11},{10,... | collective-permute-start | bytes 442376 | tf_op jit(solution)/shard_map/ppermute | solution.py:317
  44.7 7.2 %collective-permute-start.19 = (f32[256,128]{1,0:T(8,128)S(1)}, f32[256,128]{1,0:T(8,128)S(1)}, u32[]{:S(2)}, u32[]{:S(2)}) collective-permute-start(f32[256,128]{1,0:T(8,128)S(1)} %get-tuple-element.66.refs_0_), channel_id=1, source_target_pairs={{0,4},{1,5},{2,6},{3,7},{4,8},{5,9},{6,10},{7,11},{8,12},{9,13},{1... | collective-permute-start | bytes 393224 | tf_op jit(solution)/shard_map/ppermute | solution.py:317
  44.8 9.1 %collective-permute-start.20 = (f32[256,128]{1,0:T(8,128)S(1)}, f32[256,128]{1,0:T(8,128)S(1)}, u32[]{:S(2)}, u32[]{:S(2)}) collective-permute-start(f32[256,128]{1,0:T(8,128)S(1)} %get-tuple-element.66.refs_0_), channel_id=1, source_target_pairs={{0,8},{1,9},{2,10},{3,11},{4,12},{5,13},{6,14},{7,15},{8,0},{9,1},... | collective-permute-start | bytes 393224 | tf_op jit(solution)/shard_map/ppermute | solution.py:317
  47.9 7.0 %collective-permute-start.21 = (f32[256,128]{1,0:T(8,128)S(1)}, f32[256,128]{1,0:T(8,128)S(1)}, u32[]{:S(2)}, u32[]{:S(2)}) collective-permute-start(f32[256,128]{1,0:T(8,128)S(1)} %get-tuple-element.66.refs_0_), channel_id=1, source_target_pairs={{0,12},{1,13},{2,14},{3,15},{4,0},{5,1},{6,2},{7,3},{8,4},{9,5},{1... | collective-permute-start | bytes 393224 | tf_op jit(solution)/shard_map/ppermute | solution.py:317
  57.5 10.2 %collective-permute-start.22 = (f32[288,128]{1,0:T(8,128)S(1)}, f32[288,128]{1,0:T(8,128)S(1)}, u32[]{:S(2)}, u32[]{:S(2)}) collective-permute-start(f32[288,128]{1,0:T(8,128)S(1)} %get-tuple-element.82), channel_id=1, source_target_pairs={{0,16},{1,17},{2,18},{3,19},{4,20},{5,21},{6,22},{7,23},{8,24},{9,... | collective-permute-start | bytes 442376 | tf_op jit(solution)/shard_map/ppermute | solution.py:317
  67.7 9.6 %collective-permute-start.23 = (f32[288,128]{1,0:T(8,128)S(1)}, f32[288,128]{1,0:T(8,128)S(1)}, u32[]{:S(2)}, u32[]{:S(2)}) collective-permute-start(f32[288,128]{1,0:T(8,128)S(1)} %add.33.refs_0_), channel_id=1, source_target_pairs={{0,32},{1,33},{2,34},{3,35},{4,36},{5,37},{6,38},{7,39},{8,40},{9,... | collective-permute-start | bytes 442376 | tf_op jit(solution)/shard_map/ppermute | solution.py:317
  68.1 9.1 %collective-permute-start.24 = (f32[288,128]{1,0:T(8,128)S(1)}, f32[288,128]{1,0:T(8,128)S(1)}, u32[]{:S(2)}, u32[]{:S(2)}) collective-permute-start(f32[288,128]{1,0:T(8,128)S(1)} %add.33.refs_0_), channel_id=1, source_target_pairs={{0,64},{1,65},{2,66},{3,67},{4,68},{5,69},{6,70},{7,71},{8,72},{9,... | collective-permute-start | bytes 442376 | tf_op jit(solution)/shard_map/ppermute | solution.py:317
  68.6 8.9 %collective-permute-start.25 = (f32[288,128]{1,0:T(8,128)S(1)}, f32[288,128]{1,0:T(8,128)S(1)}, u32[]{:S(2)}, u32[]{:S(2)}) collective-permute-start(f32[288,128]{1,0:T(8,128)S(1)} %add.33.refs_0_), channel_id=1, source_target_pairs={{0,96},{1,97},{2,98},{3,99},{4,100},{5,101},{6,102},{7,103},{8,104... | collective-permute-start | bytes 442376 | tf_op jit(solution)/shard_map/ppermute | solution.py:317
  84.5 9.7 %collective-permute-start.27 = (f32[288,128]{1,0:T(8,128)S(1)}, f32[288,128]{1,0:T(8,128)S(1)}, u32[]{:S(2)}, u32[]{:S(2)}) collective-permute-start(f32[288,128]{1,0:T(8,128)S(1)} %get-tuple-element.89), channel_id=1, source_target_pairs={{0,4},{1,5},{2,6},{3,7},{4,8},{5,9},{6,10},{7,11},{8,12},{9,13},{1... | collective-permute-start | bytes 442376 | tf_op jit(solution)/shard_map/ppermute | solution.py:317
  86.8 7.4 %collective-permute-start.28 = (f32[288,128]{1,0:T(8,128)S(1)}, f32[288,128]{1,0:T(8,128)S(1)}, u32[]{:S(2)}, u32[]{:S(2)}) collective-permute-start(f32[288,128]{1,0:T(8,128)S(1)} %get-tuple-element.90), channel_id=1, source_target_pairs={{0,8},{1,9},{2,10},{3,11},{4,12},{5,13},{6,14},{7,15},{8,0},{9,1},... | collective-permute-start | bytes 442376 | tf_op jit(solution)/shard_map/ppermute | solution.py:317
  96.6 9.3 %collective-permute-start.30 = (f32[288,128]{1,0:T(8,128)S(1)}, f32[288,128]{1,0:T(8,128)S(1)}, u32[]{:S(2)}, u32[]{:S(2)}) collective-permute-start(f32[288,128]{1,0:T(8,128)S(1)} %add_add_fusion.after_ref.refs_0_), channel_id=1, source_target_pairs={{0,1},{1,2},{2,3},{3,0},{4,5},{5,6},{6,7},{7,4},{8,9},{9,10},{10,1... | collective-permute-start | bytes 442376 | tf_op jit(solution)/shard_map/ppermute | solution.py:317
  97.0 8.9 %collective-permute-start.31 = (f32[288,128]{1,0:T(8,128)S(1)}, f32[288,128]{1,0:T(8,128)S(1)}, u32[]{:S(2)}, u32[]{:S(2)}) collective-permute-start(f32[288,128]{1,0:T(8,128)S(1)} %add_add_fusion.after_ref.refs_0_), channel_id=1, source_target_pairs={{0,2},{1,3},{2,0},{3,1},{4,6},{5,7},{6,4},{7,5},{8,10},{9,11},{10,... | collective-permute-start | bytes 442376 | tf_op jit(solution)/shard_map/ppermute | solution.py:317
  99.7 6.3 %collective-permute-start.32 = (f32[288,128]{1,0:T(8,128)S(1)}, f32[288,128]{1,0:T(8,128)S(1)}, u32[]{:S(2)}, u32[]{:S(2)}) collective-permute-start(f32[288,128]{1,0:T(8,128)S(1)} %add_add_fusion.after_ref.refs_0_), channel_id=1, source_target_pairs={{0,3},{1,0},{2,1},{3,2},{4,7},{5,4},{6,5},{7,6},{8,11},{9,8},{10,9... | collective-permute-start | bytes 442376 | tf_op jit(solution)/shard_map/ppermute | solution.py:317
  106.0 6.8 %collective-permute-start.33 = (f32[256,128]{1,0:T(8,128)S(1)}, f32[256,128]{1,0:T(8,128)S(1)}, u32[]{:S(2)}, u32[]{:S(2)}) collective-permute-start(f32[256,128]{1,0:T(8,128)S(1)} %get-tuple-element.95.refs_0_), channel_id=1, source_target_pairs={{0,4},{1,5},{2,6},{3,7},{4,8},{5,9},{6,10},{7,11},{8,12},{9,13},{1... | collective-permute-start | bytes 393224 | tf_op jit(solution)/shard_map/ppermute | solution.py:317
  106.1 6.7 %collective-permute-start.34 = (f32[256,128]{1,0:T(8,128)S(1)}, f32[256,128]{1,0:T(8,128)S(1)}, u32[]{:S(2)}, u32[]{:S(2)}) collective-permute-start(f32[256,128]{1,0:T(8,128)S(1)} %get-tuple-element.95.refs_0_), channel_id=1, source_target_pairs={{0,8},{1,9},{2,10},{3,11},{4,12},{5,13},{6,14},{7,15},{8,0},{9,1},... | collective-permute-start | bytes 393224 | tf_op jit(solution)/shard_map/ppermute | solution.py:317
  (20 other events, 94.3 us)

commit v3 on v2

--- a/solution.py
+++ b/solution.py
@@ -48,6 +48,12 @@
     first = jnp.where(low, high, pltpu.roll(rest, RANK, 1))
     second = jnp.where(low, pltpu.roll(high, RANK, 1), rest)
     return jnp.concatenate([first, second], axis=0).astype(BF16)
+
+
+def gram_of(stack):
+    four = single(stack, stack, ((1,), (1,)))
+    two = four[:RANK] + four[RANK:]
+    return two[:, :RANK] + two[:, RANK:]
 
 
 def pack_gram(gram):
@@ -102,7 +108,7 @@
 def quarter_kernel(place_ref, *refs):
     v = place_ref[3]
     for k in range(4):
-        rows = pl.ds(pl.multiple_of(lax.rem(v + 4 - k, 4) * RANK, RANK), RANK)
+        rows = pl.ds(pl.multiple_of((v ^ k) * RANK, RANK), RANK)
         piece = refs[k][...].T
         refs[-1][rows] = jnp.concatenate([piece[:RANK], piece[RANK:]], axis=1)
 
@@ -117,7 +123,7 @@
     wide_ref, tall_ref, gram_ref, held = refs
     y, core = place_ref[0], place_ref[1]
     for k in range(4):
-        spot = lax.rem(y + 4 - k, 4) if start else k
+        spot = y ^ k if start else k
         if start:
             own, other = owns[k][...], others[k][...]
         else:
@@ -127,8 +133,8 @@
     full = jnp.concatenate([held[c] for c in range(8)], axis=1)
     if not start:
         full = exact(inv_ref[:RANK, :RANK], full, ((1,), (0,)))
-    gram_ref[...] = pack_gram(exact(full, full, ((1,), (1,))))
     high, low = two_parts(full)
+    gram_ref[...] = pack_gram(gram_of(jnp.concatenate([high, low], axis=0)))
     wide_ref[0:64] = high
     wide_ref[64:128] = high
     wide_ref[128:192] = low
@@ -143,7 +149,7 @@
 
 def rows_kernel(j, place_ref, a_ref, left_ref, wide_ref, tall_ref, gram_ref, s_ref, h_ref, l_ref):
     core, u = place_ref[1], place_ref[2]
-    q = lax.rem(u + j + 1, 4)
+    q = u ^ ((j + 1) % 4)
     low = low_lanes((RANK, PIECE))
     for half in range(2):
         spots = []
@@ -204,9 +210,9 @@
             left_refs[0][...] = jnp.concatenate([own[:, :RANK], own[:, RANK:]], axis=0).T
         turned = packed.T
         turned = jnp.concatenate([turned[:RANK], turned[RANK:]], axis=1)
-        gram += exact(turned, turned, ((1,), (1,)))
-        high, rest = two_parts(turned)
-        stacks.append(jnp.concatenate([high, rest], axis=0))
+        stack = jnp.concatenate(two_parts(turned), axis=0)
+        gram += gram_of(stack)
+        stacks.append(stack)
     tiles = []
     for t in range(4):
         cols = slice(256 * t, 256 * t + 256)
@@ -233,7 +239,7 @@
     y = place_ref[0]
     gram = first_ref[256:288] + second_ref[256:288]
     for k in range(4):
-        rows = pl.ds(pl.multiple_of(lax.rem(y + k, 4) * RANK, RANK), RANK)
+        rows = pl.ds(pl.multiple_of((y ^ k) * RANK, RANK), RANK)
         out_refs[k][0:64] = first_ref[rows] + second_ref[rows]
         out_refs[k][64:96] = gram
 
@@ -302,11 +308,11 @@
             elif kind == "v":
                 axis = "zx"[core]
             if axis == "x":
-                x = (x + k) % 4
+                x = x ^ k
             elif axis == "z":
-                z = (z + k) % 4
+                z = z ^ k
             elif axis == "y":
-                y = (y + k) % 4
+                y = y ^ k
             else:
                 core = 1 - core
             pairs.append((chan * 16 + tm, (2 * y + core) * 16 + 4 * x + z))
@@ -329,7 +335,7 @@
                 q, i = divmod(p, 4)
                 if core == 1:
                     q, i = i, q
-                spots.append((u - q) % 4 * 4 + i)
+                spots.append((u ^ q) * 4 + i)
             table[chan * 16 + tm] = [y, core, u, v] + spots
     return table
 
@@ -360,7 +366,7 @@
             s, h, r = call(
                 functools.partial(rows_kernel, j),
                 [shape(288, 128), pltpu.VMEM((512, 1024), BF16), pltpu.VMEM((512, 1024), BF16)],
-                [place, readings, lefts[3 - j], wide, tall, gram],
+                [place, readings, lefts[(j + 1) % 4], wide, tall, gram],
                 name="rows",
                 flops=2 * 512 * 1024 * 768,
             )
@@ -410,7 +416,7 @@
             name="cols_own",
             flops=2 * 512 * 1024 * 256,
         )
-        order = (2, 1, 0)
+        order = (0, 1, 2)
         outs = [shape(288, 128), shape(288, 128)] + ([] if last else [shape(256, 128)] * 3)
         mine, other, *more = call(
             functools.partial(cols_kernel, 3, True, last),

time: 131 us -> 132 us (level)
    ppermute x40, waiting for transfers between devices: 23.8 us -> 25.1 us  [send(): return lax.ppermute(values, AXES, ring(kind, k))]
  transfers between devices with their start and end apart: 40 -> 40, of which waited for: 16 -> 13; matrix products, arithmetic and copies ran while one was open for 1% -> 1% of each run, Pallas kernels for 24% -> 23%
where the time goes in v3:
time: 132 us; the launch traced here: 131 us
  starting transfers between devices  60.6 us (46%)
  Pallas kernels  43 us (33%)
  waiting for transfers between devices  25.1 us (19%)
  local copies, waits for them, and re-layouts  1.46 us (1%)
    ppermute x40, starting transfers between devices, send(): return lax.ppermute(values, AXES, ring(kind, k))  60.6 us
    pallas_call x23, Pallas kernels, call(): pl.pallas_call(kernel, out_shape=outs, in_specs=[SM if a.dtype == jnp.int...  36.8 us
    ppermute x40, waiting for transfers between devices, send(): return lax.ppermute(values, AXES, ring(kind, k))  25.1 us
    pallas_call x1, Pallas kernels, shards(): pl.pallas_call(outlier_kernel, out_shape=[shape(2048, 1024), shape(8, 128...  6.21 us
  transfers between devices with their start and end apart: 40, of which 13 were waited for; matrix products, arithmetic and copies ran while one was open for 1% of the time, Pallas kernels for 23%

profile of v3, /device:TPU:1, one launch (start us, length us, event | category | flops | bytes accessed | tf_op | source)
XLA Modules:
  0.0 131.3 jit_solution(3463079609196522525)
XLA Ops:
  0.6 2.2 %collective-permute-start.3 = (f32[64,128]{1,0:T(8,128)}, f32[64,128]{1,0:T(8,128)S(1)}, u32[]{:S(2)}, u32[]{:S(2)}) collective-permute-start(f32[64,128]{1,0:T(8,128)} %bitcast.12), channel_id=1, source_target_pairs={{0,32},{1,33},{2,34},{3,35},{4,36},{5,37},{6,38},{7,39},{8,40},{9,... | collective-permute-start | bytes 98312 | tf_op jit(solution)/shard_map/ppermute | solution.py:323
  2.8 2.6 %collective-permute-start.4 = (f32[64,128]{1,0:T(8,128)}, f32[64,128]{1,0:T(8,128)S(1)}, u32[]{:S(2)}, u32[]{:S(2)}) collective-permute-start(f32[64,128]{1,0:T(8,128)} %bitcast.13), channel_id=1, source_target_pairs={{0,64},{1,65},{2,66},{3,67},{4,68},{5,69},{6,70},{7,71},{8,72},{9,... | collective-permute-start | bytes 98312 | tf_op jit(solution)/shard_map/ppermute | solution.py:323
  6.7 2.5 %collective-permute-start.1 = (f32[64,128]{1,0:T(8,128)}, f32[64,128]{1,0:T(8,128)S(1)}, u32[]{:S(2)}, u32[]{:S(2)}) collective-permute-start(f32[64,128]{1,0:T(8,128)} %bitcast.9), channel_id=1, source_target_pairs={{0,2},{1,3},{2,0},{3,1},{4,6},{5,7},{6,4},{7,5},{8,10},{9,11},{10,... | collective-permute-start | bytes 98312 | tf_op jit(solution)/shard_map/ppermute | solution.py:323
  10.0 3.1 %collective-permute-start.6 = (f32[64,128]{1,0:T(8,128)}, f32[64,128]{1,0:T(8,128)S(1)}, u32[]{:S(2)}, u32[]{:S(2)}) collective-permute-start(f32[64,128]{1,0:T(8,128)} %bitcast.15), channel_id=1, source_target_pairs={{0,16},{1,17},{2,18},{3,19},{4,20},{5,21},{6,22},{7,23},{8,24},{9,... | collective-permute-start | bytes 98312 | tf_op jit(solution)/shard_map/ppermute | solution.py:323
  16.6 3.3 %collective-permute-start.12 = (f32[256,128]{1,0:T(8,128)S(1)}, f32[256,128]{1,0:T(8,128)S(1)}, u32[]{:S(2)}, u32[]{:S(2)}) collective-permute-start(f32[256,128]{1,0:T(8,128)S(1)} %quarter.1.left_ref), channel_id=1, source_target_pairs={{0,8},{1,9},{2,10},{3,11},{4,12},{5,13},{6,14},{7,15},{8,0},{9,1},... | collective-permute-start | bytes 393224 | tf_op jit(solution)/shard_map/ppermute | solution.py:323
  25.6 3.2 %collective-permute-start.13 = (f32[288,128]{1,0:T(8,128)S(1)}, f32[288,128]{1,0:T(8,128)S(1)}, u32[]{:S(2)}, u32[]{:S(2)}) collective-permute-start(f32[288,128]{1,0:T(8,128)S(1)} %get-tuple-element.63), channel_id=1, source_target_pairs={{0,8},{1,9},{2,10},{3,11},{4,12},{5,13},{6,14},{7,15},{8,0},{9,1},... | collective-permute-start | bytes 442376 | tf_op jit(solution)/shard_map/ppermute | solution.py:323
  33.2 3.0 %collective-permute-done.15 = f32[288,128]{1,0:T(8,128)S(1)} collective-permute-done((f32[288,128]{1,0:T(8,128)S(1)}, f32[288,128]{1,0:T(8,128)S(1)}, u32[]{:S(2)}, u32[]{:S(2)}) %collective-permute-start.15) | collective-permute-done | bytes 147488 | tf_op jit(solution)/shard_map/ppermute | solution.py:323
  37.1 2.3 %collective-permute-start.17 = (f32[288,128]{1,0:T(8,128)S(1)}, f32[288,128]{1,0:T(8,128)S(1)}, u32[]{:S(2)}, u32[]{:S(2)}) collective-permute-start(f32[288,128]{1,0:T(8,128)S(1)} %add_add_fusion.1.refs_0_), channel_id=1, source_target_pairs={{0,2},{1,3},{2,0},{3,1},{4,6},{5,7},{6,4},{7,5},{8,10},{9,11},{10,... | collective-permute-start | bytes 442376 | tf_op jit(solution)/shard_map/ppermute | solution.py:323
  40.6 2.9 %collective-permute-done.17.refs_2_ = f32[288,128]{1,0:T(8,128)S(1)} collective-permute-done((f32[288,128]{1,0:T(8,128)S(1)}, f32[288,128]{1,0:T(8,128)S(1)}, u32[]{:S(2)}, u32[]{:S(2)}) %collective-permute-start.17) | collective-permute-done | bytes 147488 | tf_op jit(solution)/shard_map/ppermute | solution.py:323
  49.1 2.0 %inverse.3.inv_ref = f32[128,128]{1,0:T(8,128)S(1)} custom-call(f32[32,128]{1,0:T(8,128)S(1)} %get-tuple-element.65.sum_ref), custom_call_target="tpu_custom_call" | custom-call | flops 1000000000 | bytes 1048576 | tf_op jit(solution)/shard_map/inverse/pallas_call | solution.py:287
  52.5 2.9 %cols_rest.2 = (f32[288,128]{1,0:T(8,128)S(1)}, f32[288,128]{1,0:T(8,128)S(1)}, f32[256,128]{1,0:T(8,128)S(1)}, f32[256,128]{1,0:T(8,128)S(1)}, f32[256,128]{1,0:T(8,128)S(1)}) custom-call(s32[20]{0:T(128)S(1)} %dynamic-slice_bitcast_fusion.place_ref.spots_ref, f32[128,128]{1,0:T(8,128)S(1)} %inverse.3.inv_ref, ...), custom_call_target="tpu_custom_call" | custom-call | flops 805306368 | bytes 1048576 | tf_op jit(solution)/shard_map/cols_rest/pallas_call | solution.py:287
  55.4 6.5 %collective-permute-start.22 = (f32[288,128]{1,0:T(8,128)S(1)}, f32[288,128]{1,0:T(8,128)S(1)}, u32[]{:S(2)}, u32[]{:S(2)}) collective-permute-start(f32[288,128]{1,0:T(8,128)S(1)} %get-tuple-element.82), channel_id=1, source_target_pairs={{0,16},{1,17},{2,18},{3,19},{4,20},{5,21},{6,22},{7,23},{8,24},{9,... | collective-permute-start | bytes 442376 | tf_op jit(solution)/shard_map/ppermute | solution.py:323
  63.1 3.8 %collective-permute-start.24 = (f32[288,128]{1,0:T(8,128)S(1)}, f32[288,128]{1,0:T(8,128)S(1)}, u32[]{:S(2)}, u32[]{:S(2)}) collective-permute-start(f32[288,128]{1,0:T(8,128)S(1)} %add.33.refs_0_), channel_id=1, source_target_pairs={{0,64},{1,65},{2,66},{3,67},{4,68},{5,69},{6,70},{7,71},{8,72},{9,... | collective-permute-start | bytes 442376 | tf_op jit(solution)/shard_map/ppermute | solution.py:323
  68.1 5.7 %collective-permute-done.24.refs_2_ = f32[288,128]{1,0:T(8,128)S(1)} collective-permute-done((f32[288,128]{1,0:T(8,128)S(1)}, f32[288,128]{1,0:T(8,128)S(1)}, u32[]{:S(2)}, u32[]{:S(2)}) %collective-permute-start.24) | collective-permute-done | bytes 147488 | tf_op jit(solution)/shard_map/ppermute | solution.py:323
  73.7 2.5 %collective-permute-done.25.refs_3_ = f32[288,128]{1,0:T(8,128)S(1)} collective-permute-done((f32[288,128]{1,0:T(8,128)S(1)}, f32[288,128]{1,0:T(8,128)S(1)}, u32[]{:S(2)}, u32[]{:S(2)}) %collective-permute-start.25) | collective-permute-done | bytes 147488 | tf_op jit(solution)/shard_map/ppermute | solution.py:323
  85.6 3.9 %collective-permute-start.28 = (f32[288,128]{1,0:T(8,128)S(1)}, f32[288,128]{1,0:T(8,128)S(1)}, u32[]{:S(2)}, u32[]{:S(2)}) collective-permute-start(f32[288,128]{1,0:T(8,128)S(1)} %get-tuple-element.90), channel_id=1, source_target_pairs={{0,8},{1,9},{2,10},{3,11},{4,12},{5,13},{6,14},{7,15},{8,0},{9,1},... | collective-permute-start | bytes 442376 | tf_op jit(solution)/shard_map/ppermute | solution.py:323
  93.7 3.5 %collective-permute-done.29 = f32[288,128]{1,0:T(8,128)S(1)} collective-permute-done((f32[288,128]{1,0:T(8,128)S(1)}, f32[288,128]{1,0:T(8,128)S(1)}, u32[]{:S(2)}, u32[]{:S(2)}) %collective-permute-start.29) | collective-permute-done | bytes 147488 | tf_op jit(solution)/shard_map/ppermute | solution.py:323
  97.3 3.4 %collective-permute-start.31 = (f32[288,128]{1,0:T(8,128)S(1)}, f32[288,128]{1,0:T(8,128)S(1)}, u32[]{:S(2)}, u32[]{:S(2)}) collective-permute-start(f32[288,128]{1,0:T(8,128)S(1)} %add_add_fusion.after_ref.refs_0_), channel_id=1, source_target_pairs={{0,2},{1,3},{2,0},{3,1},{4,6},{5,7},{6,4},{7,5},{8,10},{9,11},{10,... | collective-permute-start | bytes 442376 | tf_op jit(solution)/shard_map/ppermute | solution.py:323
  101.2 6.2 %outliers.1 = (f32[2048,1024]{1,0:T(8,128)}, f32[8,128]{1,0:T(8,128)S(1)}) custom-call(s32[20]{0:T(128)S(1)} %dynamic-slice_bitcast_fusion.place_ref.spots_ref, f32[1024,128]{1,0:T(8,128)S(1)} %pad_maximum_fusion.left_ref, bf16[256,1024]{1,0:T(8,128)(2,1)S(1)} %get-tuple-element.85.wide_ref, f32[2048,1024]{1,0:T(8,128)S(1)} %bitcast.7, ...), custom_call_target="tpu_custom_call" | custom-call | flops 1073741824 | bytes 16777216 | tf_op jit(solution)/shard_map/outliers/pallas_call | solution.py:379
  108.5 2.9 %collective-permute-start.35 = (f32[256,128]{1,0:T(8,128)S(1)}, f32[256,128]{1,0:T(8,128)S(1)}, u32[]{:S(2)}, u32[]{:S(2)}) collective-permute-start(f32[256,128]{1,0:T(8,128)S(1)} %get-tuple-element.95.refs_0_), channel_id=1, source_target_pairs={{0,12},{1,13},{2,14},{3,15},{4,8},{5,9},{6,10},{7,11},{8,4},{9,5},... | collective-permute-start | bytes 393224 | tf_op jit(solution)/shard_map/ppermute | solution.py:323
  115.3 2.9 %cols_rest.3 = (f32[288,128]{1,0:T(8,128)S(1)}, f32[288,128]{1,0:T(8,128)S(1)}) custom-call(s32[20]{0:T(128)S(1)} %dynamic-slice_bitcast_fusion.place_ref.spots_ref, f32[128,128]{1,0:T(8,128)S(1)} %inverse.5.inv_ref, f32[256,128]{1,0:T(8,128)S(1)} %collective-permute-done.33.refs_0_, f32[256,128]{1,0:T(8,128)S(1)} %collective-permute-done.34.refs_1_, ...), custom_call_target="tpu_custom_call" | custom-call | flops 805306368 | bytes 1048576 | tf_op jit(solution)/shard_map/cols_rest/pallas_call | solution.py:287
  118.2 2.8 %collective-permute-start.36 = (f32[288,128]{1,0:T(8,128)S(1)}, f32[288,128]{1,0:T(8,128)S(1)}, u32[]{:S(2)}, u32[]{:S(2)}) collective-permute-start(f32[288,128]{1,0:T(8,128)S(1)} %get-tuple-element.108), channel_id=1, source_target_pairs={{0,16},{1,17},{2,18},{3,19},{4,20},{5,21},{6,22},{7,23},{8,24},{9,... | collective-permute-start | bytes 442376 | tf_op jit(solution)/shard_map/ppermute | solution.py:323
  123.8 2.7 %collective-permute-start.39 = (f32[96,128]{1,0:T(8,128)S(1)}, f32[96,128]{1,0:T(8,128)S(1)}, u32[]{:S(2)}, u32[]{:S(2)}) collective-permute-start(f32[96,128]{1,0:T(8,128)S(1)} %get-tuple-element.112), channel_id=1, source_target_pairs={{0,96},{1,97},{2,98},{3,99},{4,100},{5,101},{6,102},{7,103},{8,104... | collective-permute-start | bytes 147464 | tf_op jit(solution)/shard_map/ppermute | solution.py:323
  128.5 2.8 %final.1 = f32[64,128]{1,0:T(8,128)} custom-call(f32[96,128]{1,0:T(8,128)S(1)} %get-tuple-element.109.m0, f32[96,128]{1,0:T(8,128)S(1)} %collective-permute-done.37.m1, f32[96,128]{1,0:T(8,128)S(1)} %collective-permute-done.38.m2, f32[96,128]{1,0:T(8,128)S(1)} %collective-permute-done.39.m3), custom_call_target="tpu_custom_call" | custom-call | bytes 1048576 | tf_op jit(solution)/shard_map/final/pallas_call | solution.py:287
  (94 shorter events, 50.8 us)
Async XLA Ops:
  0.6 8.5 %collective-permute-start.3 = (f32[64,128]{1,0:T(8,128)}, f32[64,128]{1,0:T(8,128)S(1)}, u32[]{:S(2)}, u32[]{:S(2)}) collective-permute-start(f32[64,128]{1,0:T(8,128)} %bitcast.12), channel_id=1, source_target_pairs={{0,32},{1,33},{2,34},{3,35},{4,36},{5,37},{6,38},{7,39},{8,40},{9,... | collective-permute-start | bytes 98312 | tf_op jit(solution)/shard_map/ppermute | solution.py:323
  2.8 7.2 %collective-permute-start.4 = (f32[64,128]{1,0:T(8,128)}, f32[64,128]{1,0:T(8,128)S(1)}, u32[]{:S(2)}, u32[]{:S(2)}) collective-permute-start(f32[64,128]{1,0:T(8,128)} %bitcast.13), channel_id=1, source_target_pairs={{0,64},{1,65},{2,66},{3,67},{4,68},{5,69},{6,70},{7,71},{8,72},{9,... | collective-permute-start | bytes 98312 | tf_op jit(solution)/shard_map/ppermute | solution.py:323
  5.5 7.7 %collective-permute-start.5 = (f32[64,128]{1,0:T(8,128)}, f32[64,128]{1,0:T(8,128)S(1)}, u32[]{:S(2)}, u32[]{:S(2)}) collective-permute-start(f32[64,128]{1,0:T(8,128)} %bitcast.14), channel_id=1, source_target_pairs={{0,96},{1,97},{2,98},{3,99},{4,100},{5,101},{6,102},{7,103},{8,104... | collective-permute-start | bytes 98312 | tf_op jit(solution)/shard_map/ppermute | solution.py:323
  5.5 7.8 %collective-permute-start = (f32[64,128]{1,0:T(8,128)}, f32[64,128]{1,0:T(8,128)S(1)}, u32[]{:S(2)}, u32[]{:S(2)}) collective-permute-start(f32[64,128]{1,0:T(8,128)} %bitcast.8), channel_id=1, source_target_pairs={{0,1},{1,0},{2,3},{3,2},{4,5},{5,4},{6,7},{7,6},{8,9},{9,8},{10,11... | collective-permute-start | bytes 98312 | tf_op jit(solution)/shard_map/ppermute | solution.py:323
  6.7 7.0 %collective-permute-start.1 = (f32[64,128]{1,0:T(8,128)}, f32[64,128]{1,0:T(8,128)S(1)}, u32[]{:S(2)}, u32[]{:S(2)}) collective-permute-start(f32[64,128]{1,0:T(8,128)} %bitcast.9), channel_id=1, source_target_pairs={{0,2},{1,3},{2,0},{3,1},{4,6},{5,7},{6,4},{7,5},{8,10},{9,11},{10,... | collective-permute-start | bytes 98312 | tf_op jit(solution)/shard_map/ppermute | solution.py:323
  13.1 6.8 %collective-permute-start.7 = (f32[64,128]{1,0:T(8,128)S(1)}, f32[64,128]{1,0:T(8,128)S(1)}, u32[]{:S(2)}, u32[]{:S(2)}) collective-permute-start(f32[64,128]{1,0:T(8,128)S(1)} %collective-permute-done.3.refs_4_.refs_1_), channel_id=1, source_target_pairs={{0,16},{1,17},{2,18},{3,19},{4,20},{5,21},{6,22},{7,23},{8,24},{9,... | collective-permute-start | bytes 98312 | tf_op jit(solution)/shard_map/ppermute | solution.py:323
  13.2 7.2 %collective-permute-start.8 = (f32[64,128]{1,0:T(8,128)S(1)}, f32[64,128]{1,0:T(8,128)S(1)}, u32[]{:S(2)}, u32[]{:S(2)}) collective-permute-start(f32[64,128]{1,0:T(8,128)S(1)} %collective-permute-done.4.refs_5_.refs_2_), channel_id=1, source_target_pairs={{0,16},{1,17},{2,18},{3,19},{4,20},{5,21},{6,22},{7,23},{8,24},{9,... | collective-permute-start | bytes 98312 | tf_op jit(solution)/shard_map/ppermute | solution.py:323
  13.6 6.7 %collective-permute-start.9 = (f32[64,128]{1,0:T(8,128)S(1)}, f32[64,128]{1,0:T(8,128)S(1)}, u32[]{:S(2)}, u32[]{:S(2)}) collective-permute-start(f32[64,128]{1,0:T(8,128)S(1)} %collective-permute-done.5.refs_6_.refs_3_), channel_id=1, source_target_pairs={{0,16},{1,17},{2,18},{3,19},{4,20},{5,21},{6,22},{7,23},{8,24},{9,... | collective-permute-start | bytes 98312 | tf_op jit(solution)/shard_map/ppermute | solution.py:323
  16.6 7.1 %collective-permute-start.12 = (f32[256,128]{1,0:T(8,128)S(1)}, f32[256,128]{1,0:T(8,128)S(1)}, u32[]{:S(2)}, u32[]{:S(2)}) collective-permute-start(f32[256,128]{1,0:T(8,128)S(1)} %quarter.1.left_ref), channel_id=1, source_target_pairs={{0,8},{1,9},{2,10},{3,11},{4,12},{5,13},{6,14},{7,15},{8,0},{9,1},... | collective-permute-start | bytes 393224 | tf_op jit(solution)/shard_map/ppermute | solution.py:323
  19.9 8.9 %collective-permute-start.14 = (f32[256,128]{1,0:T(8,128)S(1)}, f32[256,128]{1,0:T(8,128)S(1)}, u32[]{:S(2)}, u32[]{:S(2)}) collective-permute-start(f32[256,128]{1,0:T(8,128)S(1)} %quarter.1.left_ref), channel_id=1, source_target_pairs={{0,12},{1,13},{2,14},{3,15},{4,8},{5,9},{6,10},{7,11},{8,4},{9,5},... | collective-permute-start | bytes 393224 | tf_op jit(solution)/shard_map/ppermute | solution.py:323
  23.3 9.9 %collective-permute-start.11 = (f32[288,128]{1,0:T(8,128)S(1)}, f32[288,128]{1,0:T(8,128)S(1)}, u32[]{:S(2)}, u32[]{:S(2)}) collective-permute-start(f32[288,128]{1,0:T(8,128)S(1)} %get-tuple-element.62), channel_id=1, source_target_pairs={{0,4},{1,5},{2,6},{3,7},{4,0},{5,1},{6,2},{7,3},{8,12},{9,13},{10,... | collective-permute-start | bytes 442376 | tf_op jit(solution)/shard_map/ppermute | solution.py:323
  25.6 7.6 %collective-permute-start.13 = (f32[288,128]{1,0:T(8,128)S(1)}, f32[288,128]{1,0:T(8,128)S(1)}, u32[]{:S(2)}, u32[]{:S(2)}) collective-permute-start(f32[288,128]{1,0:T(8,128)S(1)} %get-tuple-element.63), channel_id=1, source_target_pairs={{0,8},{1,9},{2,10},{3,11},{4,12},{5,13},{6,14},{7,15},{8,0},{9,1},... | collective-permute-start | bytes 442376 | tf_op jit(solution)/shard_map/ppermute | solution.py:323
  45.1 7.3 %collective-permute-start.19 = (f32[256,128]{1,0:T(8,128)S(1)}, f32[256,128]{1,0:T(8,128)S(1)}, u32[]{:S(2)}, u32[]{:S(2)}) collective-permute-start(f32[256,128]{1,0:T(8,128)S(1)} %get-tuple-element.66.refs_0_), channel_id=1, source_target_pairs={{0,4},{1,5},{2,6},{3,7},{4,0},{5,1},{6,2},{7,3},{8,12},{9,13},{10,... | collective-permute-start | bytes 393224 | tf_op jit(solution)/shard_map/ppermute | solution.py:323
  45.2 7.3 %collective-permute-start.20 = (f32[256,128]{1,0:T(8,128)S(1)}, f32[256,128]{1,0:T(8,128)S(1)}, u32[]{:S(2)}, u32[]{:S(2)}) collective-permute-start(f32[256,128]{1,0:T(8,128)S(1)} %get-tuple-element.66.refs_0_), channel_id=1, source_target_pairs={{0,8},{1,9},{2,10},{3,11},{4,12},{5,13},{6,14},{7,15},{8,0},{9,1},... | collective-permute-start | bytes 393224 | tf_op jit(solution)/shard_map/ppermute | solution.py:323
  55.4 7.5 %collective-permute-start.22 = (f32[288,128]{1,0:T(8,128)S(1)}, f32[288,128]{1,0:T(8,128)S(1)}, u32[]{:S(2)}, u32[]{:S(2)}) collective-permute-start(f32[288,128]{1,0:T(8,128)S(1)} %get-tuple-element.82), channel_id=1, source_target_pairs={{0,16},{1,17},{2,18},{3,19},{4,20},{5,21},{6,22},{7,23},{8,24},{9,... | collective-permute-start | bytes 442376 | tf_op jit(solution)/shard_map/ppermute | solution.py:323
  63.1 10.6 %collective-permute-start.24 = (f32[288,128]{1,0:T(8,128)S(1)}, f32[288,128]{1,0:T(8,128)S(1)}, u32[]{:S(2)}, u32[]{:S(2)}) collective-permute-start(f32[288,128]{1,0:T(8,128)S(1)} %add.33.refs_0_), channel_id=1, source_target_pairs={{0,64},{1,65},{2,66},{3,67},{4,68},{5,69},{6,70},{7,71},{8,72},{9,... | collective-permute-start | bytes 442376 | tf_op jit(solution)/shard_map/ppermute | solution.py:323
  66.9 9.3 %collective-permute-start.25 = (f32[288,128]{1,0:T(8,128)S(1)}, f32[288,128]{1,0:T(8,128)S(1)}, u32[]{:S(2)}, u32[]{:S(2)}) collective-permute-start(f32[288,128]{1,0:T(8,128)S(1)} %add.33.refs_0_), channel_id=1, source_target_pairs={{0,96},{1,97},{2,98},{3,99},{4,100},{5,101},{6,102},{7,103},{8,104... | collective-permute-start | bytes 442376 | tf_op jit(solution)/shard_map/ppermute | solution.py:323
  82.7 10.9 %collective-permute-start.27 = (f32[288,128]{1,0:T(8,128)S(1)}, f32[288,128]{1,0:T(8,128)S(1)}, u32[]{:S(2)}, u32[]{:S(2)}) collective-permute-start(f32[288,128]{1,0:T(8,128)S(1)} %get-tuple-element.89), channel_id=1, source_target_pairs={{0,4},{1,5},{2,6},{3,7},{4,0},{5,1},{6,2},{7,3},{8,12},{9,13},{10,... | collective-permute-start | bytes 442376 | tf_op jit(solution)/shard_map/ppermute | solution.py:323
  85.6 8.0 %collective-permute-start.28 = (f32[288,128]{1,0:T(8,128)S(1)}, f32[288,128]{1,0:T(8,128)S(1)}, u32[]{:S(2)}, u32[]{:S(2)}) collective-permute-start(f32[288,128]{1,0:T(8,128)S(1)} %get-tuple-element.90), channel_id=1, source_target_pairs={{0,8},{1,9},{2,10},{3,11},{4,12},{5,13},{6,14},{7,15},{8,0},{9,1},... | collective-permute-start | bytes 442376 | tf_op jit(solution)/shard_map/ppermute | solution.py:323
  97.2 10.2 %collective-permute-start.30 = (f32[288,128]{1,0:T(8,128)S(1)}, f32[288,128]{1,0:T(8,128)S(1)}, u32[]{:S(2)}, u32[]{:S(2)}) collective-permute-start(f32[288,128]{1,0:T(8,128)S(1)} %add_add_fusion.after_ref.refs_0_), channel_id=1, source_target_pairs={{0,1},{1,0},{2,3},{3,2},{4,5},{5,4},{6,7},{7,6},{8,9},{9,8},{10,11... | collective-permute-start | bytes 442376 | tf_op jit(solution)/shard_map/ppermute | solution.py:323
  97.3 10.1 %collective-permute-start.31 = (f32[288,128]{1,0:T(8,128)S(1)}, f32[288,128]{1,0:T(8,128)S(1)}, u32[]{:S(2)}, u32[]{:S(2)}) collective-permute-start(f32[288,128]{1,0:T(8,128)S(1)} %add_add_fusion.after_ref.refs_0_), channel_id=1, source_target_pairs={{0,2},{1,3},{2,0},{3,1},{4,6},{5,7},{6,4},{7,5},{8,10},{9,11},{10,... | collective-permute-start | bytes 442376 | tf_op jit(solution)/shard_map/ppermute | solution.py:323
  100.7 6.7 %collective-permute-start.32 = (f32[288,128]{1,0:T(8,128)S(1)}, f32[288,128]{1,0:T(8,128)S(1)}, u32[]{:S(2)}, u32[]{:S(2)}) collective-permute-start(f32[288,128]{1,0:T(8,128)S(1)} %add_add_fusion.after_ref.refs_0_), channel_id=1, source_target_pairs={{0,3},{1,2},{2,1},{3,0},{4,7},{5,6},{6,5},{7,4},{8,11},{9,10},{10,... | collective-permute-start | bytes 442376 | tf_op jit(solution)/shard_map/ppermute | solution.py:323
  107.5 7.8 %collective-permute-start.33 = (f32[256,128]{1,0:T(8,128)S(1)}, f32[256,128]{1,0:T(8,128)S(1)}, u32[]{:S(2)}, u32[]{:S(2)}) collective-permute-start(f32[256,128]{1,0:T(8,128)S(1)} %get-tuple-element.95.refs_0_), channel_id=1, source_target_pairs={{0,4},{1,5},{2,6},{3,7},{4,0},{5,1},{6,2},{7,3},{8,12},{9,13},{10,... | collective-permute-start | bytes 393224 | tf_op jit(solution)/shard_map/ppermute | solution.py:323
  107.6 7.7 %collective-permute-start.34 = (f32[256,128]{1,0:T(8,128)S(1)}, f32[256,128]{1,0:T(8,128)S(1)}, u32[]{:S(2)}, u32[]{:S(2)}) collective-permute-start(f32[256,128]{1,0:T(8,128)S(1)} %get-tuple-element.95.refs_0_), channel_id=1, source_target_pairs={{0,8},{1,9},{2,10},{3,11},{4,12},{5,13},{6,14},{7,15},{8,0},{9,1},... | collective-permute-start | bytes 393224 | tf_op jit(solution)/shard_map/ppermute | solution.py:323
  (20 other events, 98.7 us)

commit v4 on v2

--- a/solution.py
+++ b/solution.py
@@ -48,6 +48,12 @@
     first = jnp.where(low, high, pltpu.roll(rest, RANK, 1))
     second = jnp.where(low, pltpu.roll(high, RANK, 1), rest)
     return jnp.concatenate([first, second], axis=0).astype(BF16)
+
+
+def gram_of(stack):
+    four = single(stack, stack, ((1,), (1,)))
+    two = four[:RANK] + four[RANK:]
+    return two[:, :RANK] + two[:, RANK:]
 
 
 def pack_gram(gram):
@@ -127,8 +133,8 @@
     full = jnp.concatenate([held[c] for c in range(8)], axis=1)
     if not start:
         full = exact(inv_ref[:RANK, :RANK], full, ((1,), (0,)))
-    gram_ref[...] = pack_gram(exact(full, full, ((1,), (1,))))
     high, low = two_parts(full)
+    gram_ref[...] = pack_gram(gram_of(jnp.concatenate([high, low], axis=0)))
     wide_ref[0:64] = high
     wide_ref[64:128] = high
     wide_ref[128:192] = low
@@ -204,9 +210,9 @@
             left_refs[0][...] = jnp.concatenate([own[:, :RANK], own[:, RANK:]], axis=0).T
         turned = packed.T
         turned = jnp.concatenate([turned[:RANK], turned[RANK:]], axis=1)
-        gram += exact(turned, turned, ((1,), (1,)))
-        high, rest = two_parts(turned)
-        stacks.append(jnp.concatenate([high, rest], axis=0))
+        stack = jnp.concatenate(two_parts(turned), axis=0)
+        gram += gram_of(stack) if count == 1 else exact(turned, turned, ((1,), (1,)))
+        stacks.append(stack)
     tiles = []
     for t in range(4):
         cols = slice(256 * t, 256 * t + 256)

time: 131 us -> 131 us (level)
  transfers between devices with their start and end apart: 40 -> 40, of which waited for: 16 -> 16; matrix products, arithmetic and copies ran while one was open for 1% -> 1% of each run, Pallas kernels for 24% -> 23%
where the time goes in v4:
time: 131 us; the launch traced here: 130 us
  starting transfers between devices  61.5 us (47%)
  Pallas kernels  42.3 us (32%)
  waiting for transfers between devices  24.1 us (18%)
  local copies, waits for them, and re-layouts  1.46 us (1%)
    ppermute x40, starting transfers between devices, send(): return lax.ppermute(values, AXES, ring(kind, k))  61.5 us
    pallas_call x23, Pallas kernels, call(): pl.pallas_call(kernel, out_shape=outs, in_specs=[SM if a.dtype == jnp.int...  36.1 us
    ppermute x40, waiting for transfers between devices, send(): return lax.ppermute(values, AXES, ring(kind, k))  24.1 us
    pallas_call x1, Pallas kernels, shards(): pl.pallas_call(outlier_kernel, out_shape=[shape(2048, 1024), shape(8, 128...  6.21 us
  transfers between devices with their start and end apart: 40, of which 16 were waited for; matrix products, arithmetic and copies ran while one was open for 1% of the time, Pallas kernels for 23%

profile of v4, /device:TPU:1, one launch (start us, length us, event | category | flops | bytes accessed | tf_op | source)
XLA Modules:
  0.0 130.4 jit_solution(437959719764193592)
XLA Ops:
  0.6 2.2 %collective-permute-start.3 = (f32[64,128]{1,0:T(8,128)}, f32[64,128]{1,0:T(8,128)S(1)}, u32[]{:S(2)}, u32[]{:S(2)}) collective-permute-start(f32[64,128]{1,0:T(8,128)} %bitcast.12), channel_id=1, source_target_pairs={{0,32},{1,33},{2,34},{3,35},{4,36},{5,37},{6,38},{7,39},{8,40},{9,... | collective-permute-start | bytes 98312 | tf_op jit(solution)/shard_map/ppermute | solution.py:323
  2.8 2.6 %collective-permute-start.4 = (f32[64,128]{1,0:T(8,128)}, f32[64,128]{1,0:T(8,128)S(1)}, u32[]{:S(2)}, u32[]{:S(2)}) collective-permute-start(f32[64,128]{1,0:T(8,128)} %bitcast.13), channel_id=1, source_target_pairs={{0,64},{1,65},{2,66},{3,67},{4,68},{5,69},{6,70},{7,71},{8,72},{9,... | collective-permute-start | bytes 98312 | tf_op jit(solution)/shard_map/ppermute | solution.py:323
  7.7 2.5 %collective-permute-start.1 = (f32[64,128]{1,0:T(8,128)}, f32[64,128]{1,0:T(8,128)S(1)}, u32[]{:S(2)}, u32[]{:S(2)}) collective-permute-start(f32[64,128]{1,0:T(8,128)} %bitcast.9), channel_id=1, source_target_pairs={{0,2},{1,3},{2,0},{3,1},{4,6},{5,7},{6,4},{7,5},{8,10},{9,11},{10,... | collective-permute-start | bytes 98312 | tf_op jit(solution)/shard_map/ppermute | solution.py:323
  12.0 3.2 %collective-permute-start.6 = (f32[64,128]{1,0:T(8,128)}, f32[64,128]{1,0:T(8,128)S(1)}, u32[]{:S(2)}, u32[]{:S(2)}) collective-permute-start(f32[64,128]{1,0:T(8,128)} %bitcast.15), channel_id=1, source_target_pairs={{0,16},{1,17},{2,18},{3,19},{4,20},{5,21},{6,22},{7,23},{8,24},{9,... | collective-permute-start | bytes 98312 | tf_op jit(solution)/shard_map/ppermute | solution.py:323
  26.9 2.6 %collective-permute-start.13 = (f32[288,128]{1,0:T(8,128)S(1)}, f32[288,128]{1,0:T(8,128)S(1)}, u32[]{:S(2)}, u32[]{:S(2)}) collective-permute-start(f32[288,128]{1,0:T(8,128)S(1)} %get-tuple-element.63), channel_id=1, source_target_pairs={{0,8},{1,9},{2,10},{3,11},{4,12},{5,13},{6,14},{7,15},{8,0},{9,1},... | collective-permute-start | bytes 442376 | tf_op jit(solution)/shard_map/ppermute | solution.py:323
  37.1 2.4 %collective-permute-start.17 = (f32[288,128]{1,0:T(8,128)S(1)}, f32[288,128]{1,0:T(8,128)S(1)}, u32[]{:S(2)}, u32[]{:S(2)}) collective-permute-start(f32[288,128]{1,0:T(8,128)S(1)} %add_add_fusion.1.refs_0_), channel_id=1, source_target_pairs={{0,2},{1,3},{2,0},{3,1},{4,6},{5,7},{6,4},{7,5},{8,10},{9,11},{10,... | collective-permute-start | bytes 442376 | tf_op jit(solution)/shard_map/ppermute | solution.py:323
  40.9 2.8 %collective-permute-done.17.refs_2_ = f32[288,128]{1,0:T(8,128)S(1)} collective-permute-done((f32[288,128]{1,0:T(8,128)S(1)}, f32[288,128]{1,0:T(8,128)S(1)}, u32[]{:S(2)}, u32[]{:S(2)}) %collective-permute-start.17) | collective-permute-done | bytes 147488 | tf_op jit(solution)/shard_map/ppermute | solution.py:323
  44.8 3.1 %collective-permute-start.20 = (f32[256,128]{1,0:T(8,128)S(1)}, f32[256,128]{1,0:T(8,128)S(1)}, u32[]{:S(2)}, u32[]{:S(2)}) collective-permute-start(f32[256,128]{1,0:T(8,128)S(1)} %get-tuple-element.66.refs_0_), channel_id=1, source_target_pairs={{0,8},{1,9},{2,10},{3,11},{4,12},{5,13},{6,14},{7,15},{8,0},{9,1},... | collective-permute-start | bytes 393224 | tf_op jit(solution)/shard_map/ppermute | solution.py:323
  47.9 2.0 %inverse.3.inv_ref = f32[128,128]{1,0:T(8,128)S(1)} custom-call(f32[32,128]{1,0:T(8,128)S(1)} %get-tuple-element.65.sum_ref), custom_call_target="tpu_custom_call" | custom-call | flops 1000000000 | bytes 1048576 | tf_op jit(solution)/shard_map/inverse/pallas_call | solution.py:287
  55.0 2.5 %cols_rest.2 = (f32[288,128]{1,0:T(8,128)S(1)}, f32[288,128]{1,0:T(8,128)S(1)}, f32[256,128]{1,0:T(8,128)S(1)}, f32[256,128]{1,0:T(8,128)S(1)}, f32[256,128]{1,0:T(8,128)S(1)}) custom-call(s32[20]{0:T(128)S(1)} %dynamic-slice_bitcast_fusion.place_ref.spots_ref, f32[128,128]{1,0:T(8,128)S(1)} %inverse.3.inv_ref, ...), custom_call_target="tpu_custom_call" | custom-call | flops 805306368 | bytes 1048576 | tf_op jit(solution)/shard_map/cols_rest/pallas_call | solution.py:287
  57.5 9.2 %collective-permute-start.22 = (f32[288,128]{1,0:T(8,128)S(1)}, f32[288,128]{1,0:T(8,128)S(1)}, u32[]{:S(2)}, u32[]{:S(2)}) collective-permute-start(f32[288,128]{1,0:T(8,128)S(1)} %get-tuple-element.82), channel_id=1, source_target_pairs={{0,16},{1,17},{2,18},{3,19},{4,20},{5,21},{6,22},{7,23},{8,24},{9,... | collective-permute-start | bytes 442376 | tf_op jit(solution)/shard_map/ppermute | solution.py:323
  68.7 2.0 %collective-permute-start.25 = (f32[288,128]{1,0:T(8,128)S(1)}, f32[288,128]{1,0:T(8,128)S(1)}, u32[]{:S(2)}, u32[]{:S(2)}) collective-permute-start(f32[288,128]{1,0:T(8,128)S(1)} %add.33.refs_0_), channel_id=1, source_target_pairs={{0,96},{1,97},{2,98},{3,99},{4,100},{5,101},{6,102},{7,103},{8,104... | collective-permute-start | bytes 442376 | tf_op jit(solution)/shard_map/ppermute | solution.py:323
  70.7 6.6 %collective-permute-done.23.refs_1_ = f32[288,128]{1,0:T(8,128)S(1)} collective-permute-done((f32[288,128]{1,0:T(8,128)S(1)}, f32[288,128]{1,0:T(8,128)S(1)}, u32[]{:S(2)}, u32[]{:S(2)}) %collective-permute-start.23) | collective-permute-done | bytes 147488 | tf_op jit(solution)/shard_map/ppermute | solution.py:323
  79.2 2.0 %inverse.4.refs_2_ = f32[128,128]{1,0:T(8,128)S(1)} custom-call(f32[32,128]{1,0:T(8,128)S(1)} %get-tuple-element.84.sum_ref), custom_call_target="tpu_custom_call" | custom-call | flops 1000000000 | bytes 1048576 | tf_op jit(solution)/shard_map/inverse/pallas_call | solution.py:287
  86.7 3.3 %collective-permute-start.28 = (f32[288,128]{1,0:T(8,128)S(1)}, f32[288,128]{1,0:T(8,128)S(1)}, u32[]{:S(2)}, u32[]{:S(2)}) collective-permute-start(f32[288,128]{1,0:T(8,128)S(1)} %get-tuple-element.90), channel_id=1, source_target_pairs={{0,8},{1,9},{2,10},{3,11},{4,12},{5,13},{6,14},{7,15},{8,0},{9,1},... | collective-permute-start | bytes 442376 | tf_op jit(solution)/shard_map/ppermute | solution.py:323
  94.1 2.3 %collective-permute-done.29 = f32[288,128]{1,0:T(8,128)S(1)} collective-permute-done((f32[288,128]{1,0:T(8,128)S(1)}, f32[288,128]{1,0:T(8,128)S(1)}, u32[]{:S(2)}, u32[]{:S(2)}) %collective-permute-start.29) | collective-permute-done | bytes 147488 | tf_op jit(solution)/shard_map/ppermute | solution.py:323
  96.9 2.6 %collective-permute-start.31 = (f32[288,128]{1,0:T(8,128)S(1)}, f32[288,128]{1,0:T(8,128)S(1)}, u32[]{:S(2)}, u32[]{:S(2)}) collective-permute-start(f32[288,128]{1,0:T(8,128)S(1)} %add_add_fusion.after_ref.refs_0_), channel_id=1, source_target_pairs={{0,2},{1,3},{2,0},{3,1},{4,6},{5,7},{6,4},{7,5},{8,10},{9,11},{10,... | collective-permute-start | bytes 442376 | tf_op jit(solution)/shard_map/ppermute | solution.py:323
  99.5 6.2 %outliers.1 = (f32[2048,1024]{1,0:T(8,128)}, f32[8,128]{1,0:T(8,128)S(1)}) custom-call(s32[20]{0:T(128)S(1)} %dynamic-slice_bitcast_fusion.place_ref.spots_ref, f32[1024,128]{1,0:T(8,128)S(1)} %pad_maximum_fusion.left_ref, bf16[256,1024]{1,0:T(8,128)(2,1)S(1)} %get-tuple-element.85.wide_ref, f32[2048,1024]{1,0:T(8,128)S(1)} %bitcast.7, ...), custom_call_target="tpu_custom_call" | custom-call | flops 1073741824 | bytes 16777216 | tf_op jit(solution)/shard_map/outliers/pallas_call | solution.py:379
  105.9 2.7 %collective-permute-start.34 = (f32[256,128]{1,0:T(8,128)S(1)}, f32[256,128]{1,0:T(8,128)S(1)}, u32[]{:S(2)}, u32[]{:S(2)}) collective-permute-start(f32[256,128]{1,0:T(8,128)S(1)} %get-tuple-element.95.refs_0_), channel_id=1, source_target_pairs={{0,8},{1,9},{2,10},{3,11},{4,12},{5,13},{6,14},{7,15},{8,0},{9,1},... | collective-permute-start | bytes 393224 | tf_op jit(solution)/shard_map/ppermute | solution.py:323
  108.6 2.0 %inverse.5.inv_ref = f32[128,128]{1,0:T(8,128)S(1)} custom-call(f32[32,128]{1,0:T(8,128)S(1)} %get-tuple-element.94.sum_ref), custom_call_target="tpu_custom_call" | custom-call | flops 1000000000 | bytes 1048576 | tf_op jit(solution)/shard_map/inverse/pallas_call | solution.py:287
  113.2 2.5 %cols_rest.3 = (f32[288,128]{1,0:T(8,128)S(1)}, f32[288,128]{1,0:T(8,128)S(1)}) custom-call(s32[20]{0:T(128)S(1)} %dynamic-slice_bitcast_fusion.place_ref.spots_ref, f32[128,128]{1,0:T(8,128)S(1)} %inverse.5.inv_ref, f32[256,128]{1,0:T(8,128)S(1)} %collective-permute-done.33.refs_0_, f32[256,128]{1,0:T(8,128)S(1)} %collective-permute-done.34.refs_1_, ...), custom_call_target="tpu_custom_call" | custom-call | flops 805306368 | bytes 1048576 | tf_op jit(solution)/shard_map/cols_rest/pallas_call | solution.py:287
  115.8 3.5 %collective-permute-start.36 = (f32[288,128]{1,0:T(8,128)S(1)}, f32[288,128]{1,0:T(8,128)S(1)}, u32[]{:S(2)}, u32[]{:S(2)}) collective-permute-start(f32[288,128]{1,0:T(8,128)S(1)} %get-tuple-element.108), channel_id=1, source_target_pairs={{0,16},{1,17},{2,18},{3,19},{4,20},{5,21},{6,22},{7,23},{8,24},{9,... | collective-permute-start | bytes 442376 | tf_op jit(solution)/shard_map/ppermute | solution.py:323
  121.1 3.3 %collective-permute-start.38 = (f32[96,128]{1,0:T(8,128)S(1)}, f32[96,128]{1,0:T(8,128)S(1)}, u32[]{:S(2)}, u32[]{:S(2)}) collective-permute-start(f32[96,128]{1,0:T(8,128)S(1)} %get-tuple-element.111), channel_id=1, source_target_pairs={{0,64},{1,65},{2,66},{3,67},{4,68},{5,69},{6,70},{7,71},{8,72},{9,... | collective-permute-start | bytes 147464 | tf_op jit(solution)/shard_map/ppermute | solution.py:323
  127.6 2.8 %final.1 = f32[64,128]{1,0:T(8,128)} custom-call(f32[96,128]{1,0:T(8,128)S(1)} %get-tuple-element.109.m0, f32[96,128]{1,0:T(8,128)S(1)} %collective-permute-done.37.m1, f32[96,128]{1,0:T(8,128)S(1)} %collective-permute-done.38.m2, f32[96,128]{1,0:T(8,128)S(1)} %collective-permute-done.39.m3), custom_call_target="tpu_custom_call" | custom-call | bytes 1048576 | tf_op jit(solution)/shard_map/final/pallas_call | solution.py:287
  (94 shorter events, 52.5 us)
Async XLA Ops:
  0.6 9.6 %collective-permute-start.3 = (f32[64,128]{1,0:T(8,128)}, f32[64,128]{1,0:T(8,128)S(1)}, u32[]{:S(2)}, u32[]{:S(2)}) collective-permute-start(f32[64,128]{1,0:T(8,128)} %bitcast.12), channel_id=1, source_target_pairs={{0,32},{1,33},{2,34},{3,35},{4,36},{5,37},{6,38},{7,39},{8,40},{9,... | collective-permute-start | bytes 98312 | tf_op jit(solution)/shard_map/ppermute | solution.py:323
  2.8 9.2 %collective-permute-start.4 = (f32[64,128]{1,0:T(8,128)}, f32[64,128]{1,0:T(8,128)S(1)}, u32[]{:S(2)}, u32[]{:S(2)}) collective-permute-start(f32[64,128]{1,0:T(8,128)} %bitcast.13), channel_id=1, source_target_pairs={{0,64},{1,65},{2,66},{3,67},{4,68},{5,69},{6,70},{7,71},{8,72},{9,... | collective-permute-start | bytes 98312 | tf_op jit(solution)/shard_map/ppermute | solution.py:323
  5.4 9.8 %collective-permute-start.5 = (f32[64,128]{1,0:T(8,128)}, f32[64,128]{1,0:T(8,128)S(1)}, u32[]{:S(2)}, u32[]{:S(2)}) collective-permute-start(f32[64,128]{1,0:T(8,128)} %bitcast.14), channel_id=1, source_target_pairs={{0,96},{1,97},{2,98},{3,99},{4,100},{5,101},{6,102},{7,103},{8,104... | collective-permute-start | bytes 98312 | tf_op jit(solution)/shard_map/ppermute | solution.py:323
  6.5 8.8 %collective-permute-start = (f32[64,128]{1,0:T(8,128)}, f32[64,128]{1,0:T(8,128)S(1)}, u32[]{:S(2)}, u32[]{:S(2)}) collective-permute-start(f32[64,128]{1,0:T(8,128)} %bitcast.8), channel_id=1, source_target_pairs={{0,1},{1,2},{2,3},{3,0},{4,5},{5,6},{6,7},{7,4},{8,9},{9,10},{10,1... | collective-permute-start | bytes 98312 | tf_op jit(solution)/shard_map/ppermute | solution.py:323
  7.7 8.0 %collective-permute-start.1 = (f32[64,128]{1,0:T(8,128)}, f32[64,128]{1,0:T(8,128)S(1)}, u32[]{:S(2)}, u32[]{:S(2)}) collective-permute-start(f32[64,128]{1,0:T(8,128)} %bitcast.9), channel_id=1, source_target_pairs={{0,2},{1,3},{2,0},{3,1},{4,6},{5,7},{6,4},{7,5},{8,10},{9,11},{10,... | collective-permute-start | bytes 98312 | tf_op jit(solution)/shard_map/ppermute | solution.py:323
  12.0 7.0 %collective-permute-start.6 = (f32[64,128]{1,0:T(8,128)}, f32[64,128]{1,0:T(8,128)S(1)}, u32[]{:S(2)}, u32[]{:S(2)}) collective-permute-start(f32[64,128]{1,0:T(8,128)} %bitcast.15), channel_id=1, source_target_pairs={{0,16},{1,17},{2,18},{3,19},{4,20},{5,21},{6,22},{7,23},{8,24},{9,... | collective-permute-start | bytes 98312 | tf_op jit(solution)/shard_map/ppermute | solution.py:323
  20.6 8.9 %collective-permute-start.14 = (f32[256,128]{1,0:T(8,128)S(1)}, f32[256,128]{1,0:T(8,128)S(1)}, u32[]{:S(2)}, u32[]{:S(2)}) collective-permute-start(f32[256,128]{1,0:T(8,128)S(1)} %quarter.1.left_ref), channel_id=1, source_target_pairs={{0,4},{1,5},{2,6},{3,7},{4,8},{5,9},{6,10},{7,11},{8,12},{9,13},{1... | collective-permute-start | bytes 393224 | tf_op jit(solution)/shard_map/ppermute | solution.py:323
  24.3 10.3 %collective-permute-start.11 = (f32[288,128]{1,0:T(8,128)S(1)}, f32[288,128]{1,0:T(8,128)S(1)}, u32[]{:S(2)}, u32[]{:S(2)}) collective-permute-start(f32[288,128]{1,0:T(8,128)S(1)} %get-tuple-element.62), channel_id=1, source_target_pairs={{0,4},{1,5},{2,6},{3,7},{4,8},{5,9},{6,10},{7,11},{8,12},{9,13},{1... | collective-permute-start | bytes 442376 | tf_op jit(solution)/shard_map/ppermute | solution.py:323
  26.9 7.7 %collective-permute-start.13 = (f32[288,128]{1,0:T(8,128)S(1)}, f32[288,128]{1,0:T(8,128)S(1)}, u32[]{:S(2)}, u32[]{:S(2)}) collective-permute-start(f32[288,128]{1,0:T(8,128)S(1)} %get-tuple-element.63), channel_id=1, source_target_pairs={{0,8},{1,9},{2,10},{3,11},{4,12},{5,13},{6,14},{7,15},{8,0},{9,1},... | collective-permute-start | bytes 442376 | tf_op jit(solution)/shard_map/ppermute | solution.py:323
  37.1 6.6 %collective-permute-start.17 = (f32[288,128]{1,0:T(8,128)S(1)}, f32[288,128]{1,0:T(8,128)S(1)}, u32[]{:S(2)}, u32[]{:S(2)}) collective-permute-start(f32[288,128]{1,0:T(8,128)S(1)} %add_add_fusion.1.refs_0_), channel_id=1, source_target_pairs={{0,2},{1,3},{2,0},{3,1},{4,6},{5,7},{6,4},{7,5},{8,10},{9,11},{10,... | collective-permute-start | bytes 442376 | tf_op jit(solution)/shard_map/ppermute | solution.py:323
  44.7 7.3 %collective-permute-start.19 = (f32[256,128]{1,0:T(8,128)S(1)}, f32[256,128]{1,0:T(8,128)S(1)}, u32[]{:S(2)}, u32[]{:S(2)}) collective-permute-start(f32[256,128]{1,0:T(8,128)S(1)} %get-tuple-element.66.refs_0_), channel_id=1, source_target_pairs={{0,4},{1,5},{2,6},{3,7},{4,8},{5,9},{6,10},{7,11},{8,12},{9,13},{1... | collective-permute-start | bytes 393224 | tf_op jit(solution)/shard_map/ppermute | solution.py:323
  44.8 9.1 %collective-permute-start.20 = (f32[256,128]{1,0:T(8,128)S(1)}, f32[256,128]{1,0:T(8,128)S(1)}, u32[]{:S(2)}, u32[]{:S(2)}) collective-permute-start(f32[256,128]{1,0:T(8,128)S(1)} %get-tuple-element.66.refs_0_), channel_id=1, source_target_pairs={{0,8},{1,9},{2,10},{3,11},{4,12},{5,13},{6,14},{7,15},{8,0},{9,1},... | collective-permute-start | bytes 393224 | tf_op jit(solution)/shard_map/ppermute | solution.py:323
  47.9 7.0 %collective-permute-start.21 = (f32[256,128]{1,0:T(8,128)S(1)}, f32[256,128]{1,0:T(8,128)S(1)}, u32[]{:S(2)}, u32[]{:S(2)}) collective-permute-start(f32[256,128]{1,0:T(8,128)S(1)} %get-tuple-element.66.refs_0_), channel_id=1, source_target_pairs={{0,12},{1,13},{2,14},{3,15},{4,0},{5,1},{6,2},{7,3},{8,4},{9,5},{1... | collective-permute-start | bytes 393224 | tf_op jit(solution)/shard_map/ppermute | solution.py:323
  57.5 10.2 %collective-permute-start.22 = (f32[288,128]{1,0:T(8,128)S(1)}, f32[288,128]{1,0:T(8,128)S(1)}, u32[]{:S(2)}, u32[]{:S(2)}) collective-permute-start(f32[288,128]{1,0:T(8,128)S(1)} %get-tuple-element.82), channel_id=1, source_target_pairs={{0,16},{1,17},{2,18},{3,19},{4,20},{5,21},{6,22},{7,23},{8,24},{9,... | collective-permute-start | bytes 442376 | tf_op jit(solution)/shard_map/ppermute | solution.py:323
  67.7 9.5 %collective-permute-start.23 = (f32[288,128]{1,0:T(8,128)S(1)}, f32[288,128]{1,0:T(8,128)S(1)}, u32[]{:S(2)}, u32[]{:S(2)}) collective-permute-start(f32[288,128]{1,0:T(8,128)S(1)} %add.33.refs_0_), channel_id=1, source_target_pairs={{0,32},{1,33},{2,34},{3,35},{4,36},{5,37},{6,38},{7,39},{8,40},{9,... | collective-permute-start | bytes 442376 | tf_op jit(solution)/shard_map/ppermute | solution.py:323
  68.2 9.1 %collective-permute-start.24 = (f32[288,128]{1,0:T(8,128)S(1)}, f32[288,128]{1,0:T(8,128)S(1)}, u32[]{:S(2)}, u32[]{:S(2)}) collective-permute-start(f32[288,128]{1,0:T(8,128)S(1)} %add.33.refs_0_), channel_id=1, source_target_pairs={{0,64},{1,65},{2,66},{3,67},{4,68},{5,69},{6,70},{7,71},{8,72},{9,... | collective-permute-start | bytes 442376 | tf_op jit(solution)/shard_map/ppermute | solution.py:323
  68.7 8.9 %collective-permute-start.25 = (f32[288,128]{1,0:T(8,128)S(1)}, f32[288,128]{1,0:T(8,128)S(1)}, u32[]{:S(2)}, u32[]{:S(2)}) collective-permute-start(f32[288,128]{1,0:T(8,128)S(1)} %add.33.refs_0_), channel_id=1, source_target_pairs={{0,96},{1,97},{2,98},{3,99},{4,100},{5,101},{6,102},{7,103},{8,104... | collective-permute-start | bytes 442376 | tf_op jit(solution)/shard_map/ppermute | solution.py:323
  84.4 9.7 %collective-permute-start.27 = (f32[288,128]{1,0:T(8,128)S(1)}, f32[288,128]{1,0:T(8,128)S(1)}, u32[]{:S(2)}, u32[]{:S(2)}) collective-permute-start(f32[288,128]{1,0:T(8,128)S(1)} %get-tuple-element.89), channel_id=1, source_target_pairs={{0,4},{1,5},{2,6},{3,7},{4,8},{5,9},{6,10},{7,11},{8,12},{9,13},{1... | collective-permute-start | bytes 442376 | tf_op jit(solution)/shard_map/ppermute | solution.py:323
  86.7 7.5 %collective-permute-start.28 = (f32[288,128]{1,0:T(8,128)S(1)}, f32[288,128]{1,0:T(8,128)S(1)}, u32[]{:S(2)}, u32[]{:S(2)}) collective-permute-start(f32[288,128]{1,0:T(8,128)S(1)} %get-tuple-element.90), channel_id=1, source_target_pairs={{0,8},{1,9},{2,10},{3,11},{4,12},{5,13},{6,14},{7,15},{8,0},{9,1},... | collective-permute-start | bytes 442376 | tf_op jit(solution)/shard_map/ppermute | solution.py:323
  96.5 9.3 %collective-permute-start.30 = (f32[288,128]{1,0:T(8,128)S(1)}, f32[288,128]{1,0:T(8,128)S(1)}, u32[]{:S(2)}, u32[]{:S(2)}) collective-permute-start(f32[288,128]{1,0:T(8,128)S(1)} %add_add_fusion.after_ref.refs_0_), channel_id=1, source_target_pairs={{0,1},{1,2},{2,3},{3,0},{4,5},{5,6},{6,7},{7,4},{8,9},{9,10},{10,1... | collective-permute-start | bytes 442376 | tf_op jit(solution)/shard_map/ppermute | solution.py:323
  96.9 8.9 %collective-permute-start.31 = (f32[288,128]{1,0:T(8,128)S(1)}, f32[288,128]{1,0:T(8,128)S(1)}, u32[]{:S(2)}, u32[]{:S(2)}) collective-permute-start(f32[288,128]{1,0:T(8,128)S(1)} %add_add_fusion.after_ref.refs_0_), channel_id=1, source_target_pairs={{0,2},{1,3},{2,0},{3,1},{4,6},{5,7},{6,4},{7,5},{8,10},{9,11},{10,... | collective-permute-start | bytes 442376 | tf_op jit(solution)/shard_map/ppermute | solution.py:323
  99.5 6.3 %collective-permute-start.32 = (f32[288,128]{1,0:T(8,128)S(1)}, f32[288,128]{1,0:T(8,128)S(1)}, u32[]{:S(2)}, u32[]{:S(2)}) collective-permute-start(f32[288,128]{1,0:T(8,128)S(1)} %add_add_fusion.after_ref.refs_0_), channel_id=1, source_target_pairs={{0,3},{1,0},{2,1},{3,2},{4,7},{5,4},{6,5},{7,6},{8,11},{9,8},{10,9... | collective-permute-start | bytes 442376 | tf_op jit(solution)/shard_map/ppermute | solution.py:323
  105.8 6.6 %collective-permute-start.33 = (f32[256,128]{1,0:T(8,128)S(1)}, f32[256,128]{1,0:T(8,128)S(1)}, u32[]{:S(2)}, u32[]{:S(2)}) collective-permute-start(f32[256,128]{1,0:T(8,128)S(1)} %get-tuple-element.95.refs_0_), channel_id=1, source_target_pairs={{0,4},{1,5},{2,6},{3,7},{4,8},{5,9},{6,10},{7,11},{8,12},{9,13},{1... | collective-permute-start | bytes 393224 | tf_op jit(solution)/shard_map/ppermute | solution.py:323
  105.9 6.6 %collective-permute-start.34 = (f32[256,128]{1,0:T(8,128)S(1)}, f32[256,128]{1,0:T(8,128)S(1)}, u32[]{:S(2)}, u32[]{:S(2)}) collective-permute-start(f32[256,128]{1,0:T(8,128)S(1)} %get-tuple-element.95.refs_0_), channel_id=1, source_target_pairs={{0,8},{1,9},{2,10},{3,11},{4,12},{5,13},{6,14},{7,15},{8,0},{9,1},... | collective-permute-start | bytes 393224 | tf_op jit(solution)/shard_map/ppermute | solution.py:323
  (20 other events, 94.4 us)
